TPU v7x, 128 devices: a whole 4x4x4 slice. The times are simulated.
128 devices in a mesh: row: 8 (over z_lo, x), col: 16 (over y, z_hi, core).
Axes of the slice: x: 4, y: 4, z: 4 (z_hi: 2, z_lo: 2; z = z_hi * 2 + z_lo), core: 2. Of those that a mesh axis runs over, the one named last changes fastest.
Arguments:
- activations: bfloat16 [2, 256, 512, 256], P(None, 'row', 'col'), may hold values from -6 to 6
- cotangent: bfloat16 [2, 256, 512, 256], P(None, 'row', 'col'), may hold values from -6 to 6
- ln_gain: float32 [256], replicated, may hold values from 0.1 to 1.9
- qkv_weight: bfloat16 [256, 768], replicated, may hold values from -0.375 to 0.375
- out_weight: bfloat16 [256, 256], replicated, may hold values from -0.375 to 0.375
- position_bias: float32 [8, 64, 64], replicated, may hold values from -300 to 300
Outputs:
- grad_input: bfloat16 [2, 256, 512, 256], P(None, 'row', 'col')
- grad_gain: float32 [256], replicated
- grad_qkv: float32 [256, 768], replicated
- grad_proj: float32 [256, 256], replicated
- grad_bias: float32 [8, 64, 64], replicated
All inputs are finite; a program needn't handle non-finite values.
Results may differ from a plain program's by a relative error of at most 0.01.
Values may be sent and summed in bfloat16 or wider, within the bound.
No kernel may reach another device: no remote copies, remote signals or barrier semaphores. Data moves between devices by JAX's collectives and lax.ppermute only.
A program may use at most 128 MiB of HBM per device.

v0:
```python
import functools, math
import jax, jax.numpy as jnp
from jax import lax
from jax.experimental import pallas as pl
from jax.experimental.pallas import tpu as pltpu
from jax.sharding import PartitionSpec as P
F32=jnp.float32; BF=jnp.bfloat16
SC=32**-0.5; L2E=math.log2(math.e)
NT=(((1,),(1,)),((),())); TN=(((0,),(0,)),((),())); NN=(((1,),(0,)),((),()))
def dg(a,b,d): return lax.dot_general(a,b,d,preferred_element_type=F32)
def layer_kernel(NB,recv,gain,wqkv,wout,bias,msg,xf0,xf1,dyf0,dyf1,biasT,dbias,gqkv,gproj,ggain):
    def cvt(s,_):
        t=recv[s]
        for i,ref in enumerate((xf0,xf1,dyf0,dyf1)):
            ref[pl.ds(s*32,32),:]=t[:,128*i:128*i+128].astype(F32)
        return 0
    lax.fori_loop(0,64,cvt,0,unroll=8)
    for q in range(4):
        biasT[:,128*q:128*(q+1)]=(bias[128*q:128*(q+1),:]*L2E).T
    dbias[...]=jnp.zeros_like(dbias); gqkv[...]=jnp.zeros_like(gqkv); gproj[...]=jnp.zeros_like(gproj); ggain[...]=jnp.zeros_like(ggain)
    lane=lax.broadcasted_iota(jnp.int32,(64,128),1)//32
    masks=[lane==h for h in range(4)]
    zero=jnp.zeros((64,128),BF)
    def expand(a):
        return jnp.concatenate([jnp.where(m,a,zero) for m in masks],axis=0)
    def pick(r):
        o=r[0:64]
        for h in range(1,4): o=jnp.where(masks[h],r[64*h:64*h+64],o)
        return o
    w=wqkv[...]; wo=wout[...]; gn=gain[...]
    def block(b,_):
        def grouped(lo,hi):
            return jnp.concatenate([jnp.concatenate([ref[pl.ds(b*NB+k,64,stride=32),:] for k in range(NB)],0) for ref in (lo,hi)],1)
        x=grouped(xf0,xf1); dy=grouped(dyf0,dyf1)
        c=x-jnp.mean(x,-1,keepdims=True)
        inv=lax.rsqrt(jnp.mean(c*c,-1,keepdims=True)+1e-5)
        normal=c*inv
        normed=(normal*gn).astype(BF)
        packed=dg(normed,w,NN)
        Q=(packed[:,:256]*(SC*L2E)).astype(BF); K=packed[:,256:512].astype(BF); V=packed[:,512:].astype(BF)
        dyb=dy.astype(BF)
        dA=dg(dyb,wo,NT).astype(BF)
        att=[];gp=[];db=[None,None]
        for k in range(NB):
            r=slice(64*k,64*k+64)
            aH=[];gq=[];gk=[];gv=[]
            for hf in range(2):
                l=slice(128*hf,128*hf+128)
                q=Q[r,l];kk=K[r,l];v=V[r,l];da=dA[r,l]
                qx=expand(q);dax=expand(da)
                t=dg(kk,qx,NT)+biasT[:,256*hf:256*hf+256]
                m=jnp.max(t,0,keepdims=True)
                e=jnp.exp2(t-m)
                p=e*(1.0/jnp.sum(e,0,keepdims=True))
                pb=p.astype(BF)
                dp=dg(v,dax,NT)
                D=jnp.sum(dp*p,0,keepdims=True)
                s=p*(dp-D)
                sb=s.astype(BF)
                db[hf]=s if db[hf] is None else db[hf]+s
                aH.append(pick(dg(pb,v,TN)).astype(BF))
                gv.append(dg(pb,dax,NN).astype(BF))
                gk.append((dg(sb,qx,NN)*(1.0/L2E)).astype(BF))
                gq.append((pick(dg(sb,kk,TN))*SC).astype(BF))
            att.append(jnp.concatenate(aH,1))
            gp.append(jnp.concatenate(gq+gk+gv,1))
        for hf in range(2): dbias[:,256*hf:256*hf+256]+=db[hf]
        A=jnp.concatenate(att,0); G=jnp.concatenate(gp,0)
        gqkv[...]+=dg(normed,G,TN)
        gproj[...]+=dg(A,dyb,TN)
        gN=dg(G,w,NT)
        gx=gN*normal
        ggain[...]+=jnp.sum(gx.reshape(-1,8,256),0)
        g=gN*gn
        dx=dy+inv*(g-jnp.mean(g,-1,keepdims=True)-normal*jnp.mean(gx*gn,-1,keepdims=True))
        for k in range(NB):
            xf0[pl.ds(b*NB+k,64,stride=32),:]=dx[64*k:64*k+64,:128]
            xf1[pl.ds(b*NB+k,64,stride=32),:]=dx[64*k:64*k+64,128:]
        return 0
    lax.fori_loop(0,32//NB,block,0)
    def wr(s,_):
        for i,ref in enumerate((xf0,xf1)):
            t=ref[pl.ds(s*32,32),:].astype(BF)
            msg[s,:,128*i:128*i+128]=t[:16]
            msg[s,:,256+128*i:384+128*i]=t[16:]
        return 0
    lax.fori_loop(0,64,wr,0,unroll=8)
    for rb in range(16):
        rr=slice(16*rb,16*rb+16)
        msg[rb*3,:,512:896]=gqkv[rr,0:384].astype(BF)
        msg[rb*3+1,:,512:896]=gqkv[rr,384:768].astype(BF)
        msg[rb*3+2,:,512:768]=gproj[rr,:].astype(BF)
        q=rb//4; j0=16*(rb%4)
        msg[rb*3+2,:,768:896]=dbias[j0:j0+16,128*q:128*q+128].astype(BF)
    msg[48:64,:,512:896]=jnp.zeros((16,16,384),BF)
    gs=jnp.sum(ggain[...],0,keepdims=True)
    msg[48,:,512:768]=jnp.broadcast_to(gs,(16,256)).astype(BF)
def layer(recv,gain,wqkv,wout,bias,NB=4):
    vm=pl.BlockSpec(memory_space=pltpu.VMEM)
    return pl.pallas_call(functools.partial(layer_kernel,NB),
        out_shape=jax.ShapeDtypeStruct((64,16,896),BF),
        in_specs=[vm]*5,out_specs=vm,
        scratch_shapes=[*[pltpu.VMEM((2048,128),F32)]*4,pltpu.VMEM((64,512),F32),pltpu.VMEM((64,512),F32),
            pltpu.VMEM((256,768),F32),pltpu.VMEM((256,256),F32),pltpu.VMEM((8,256),F32)],
        compiler_params=pltpu.CompilerParams(vmem_limit_bytes=48*2**20),
        name="grid_attention_grads")(recv,gain.reshape(1,256),wqkv,wout,bias.reshape(512,64))


def finish_kernel(y, qkv, proj, bias, gain):
    for rb in range(16):
        rr = slice(16 * rb, 16 * rb + 16)
        qkv[rr, 0:384] = y[rb * 3].astype(F32)
        qkv[rr, 384:768] = y[rb * 3 + 1].astype(F32)
        proj[rr, :] = y[rb * 3 + 2, :, 0:256].astype(F32)
    for q in range(4):
        t = jnp.concatenate([y[(q * 4 + r) * 3 + 2, :, 256:384].astype(F32) for r in range(4)], 0)
        bias[128 * q : 128 * q + 128, :] = t.T
    gain[...] = y[48, 0:1, 0:256].astype(F32)


def finish(y):
    vm = pl.BlockSpec(memory_space=pltpu.VMEM)
    return pl.pallas_call(
        finish_kernel,
        out_shape=(
            jax.ShapeDtypeStruct((256, 768), F32),
            jax.ShapeDtypeStruct((256, 256), F32),
            jax.ShapeDtypeStruct((512, 64), F32),
            jax.ShapeDtypeStruct((1, 256), F32),
        ),
        in_specs=[vm],
        out_specs=(vm,) * 4,
        name="parameter_grads",
    )(y)


CHIPS = ("zl", "x", "y", "zh")


def on_device(activations, cotangent, ln_gain, qkv_weight, out_weight, position_bias):
    both = jnp.concatenate(
        [activations.reshape(64, 32, 256), cotangent.reshape(64, 32, 256)], axis=2
    )
    arrived = lax.all_to_all(both, CHIPS, 0, 0, tiled=True)
    message = layer(arrived, ln_gain, qkv_weight, out_weight, position_bias)
    returned = lax.all_to_all(message, CHIPS, 0, 0, tiled=True)
    partial = jnp.sum(returned[:, :, 512:].astype(F32), axis=0)
    other = lax.ppermute(partial, "core", [(0, 1), (1, 0)])
    total = jnp.broadcast_to((partial + other).astype(BF)[None], (64, 16, 384))
    totals = lax.all_to_all(total, CHIPS, 0, 0, tiled=True)
    grad_input = returned[:, :, :512].reshape(64, 16, 2, 256).transpose(0, 2, 1, 3)
    grad_input = grad_input.reshape(activations.shape)
    grad_qkv, grad_proj, grad_bias, grad_gain = finish(totals)
    return (
        grad_input,
        grad_gain.reshape(256),
        grad_qkv,
        grad_proj,
        grad_bias.reshape(8, 64, 64),
    )


def solution(mesh):
    fine = jax.sharding.Mesh(mesh.devices.reshape(2, 4, 4, 2, 2), ("zl", "x", "y", "zh", "core"))
    tokens = P(None, ("zl", "x"), ("y", "zh", "core"), None)
    return jax.shard_map(
        on_device,
        mesh=fine,
        in_specs=(tokens, tokens, P(), P(), P(), P()),
        out_specs=(tokens, P(), P(), P(), P()),
        check_vma=False,
    )
```

profile of v0, /device:TPU:0, one launch (start us, length us, event | category | flops | bytes accessed | tf_op | source)
XLA Modules:
  0.0 130.5 jit_solution(18197311918358970423)
XLA Ops:
  0.6 1.7 %pad_maximum_fusion = bf16[64,32,512]{2,1,0:T(8,128)(2,1)S(1)} fusion(bf16[64,32,256]{2,1,0:T(8,128)(2,1)} %bitcast.12, bf16[64,32,256]{2,1,0:T(8,128)(2,1)} %bitcast.13), kind=kLoop, calls=%fused_computation | loop fusion | flops 4194304 | bytes 4194304 | tf_op jit(solution)/shard_map/concatenate | solution.py:141
  2.3 0.0 copy-start
  2.4 0.0 copy-start.1
  2.4 0.0 copy-start.2
  2.4 0.0 copy-start.3
  2.4 41.2 %all_to_all.15.recv = bf16[64,32,512]{2,1,0:T(8,128)(2,1)S(1)} all-to-all(bf16[64,32,512]{2,1,0:T(8,128)(2,1)S(1)} %pad_maximum_fusion), channel_id=1, replica_groups=mesh['zl'=2,'x'=4,'y'=4,'zh'=2,'core'=2] {'zl','x','y','zh'}, dimensions={0} | all-to-all | bytes 4194304 | tf_op jit(solution)/shard_map/all_to_all | solution.py:144
  43.5 0.0 copy-done
  43.5 0.0 copy-done.1
  43.5 0.0 copy-done.2
  43.6 0.0 copy-done.3
  43.6 29.8 %grid_attention_grads.1 = bf16[64,16,896]{2,1,0:T(8,128)(2,1)S(1)} custom-call(bf16[64,32,512]{2,1,0:T(8,128)(2,1)S(1)} %all_to_all.15.recv, f32[1,256]{1,0:T(1,128)S(1)} %bitcast.9, bf16[256,768]{1,0:T(8,128)(2,1)S(1)} %copy-done, bf16[256,256]{1,0:T(8,128)(2,1)S(1)} %copy-done.2, f32[512,64]{1,0:T(8,128)S(1)} %bitcast.8), custom_call_target="tpu_custom_call" | custom-call | tf_op jit(solution)/shard_map/grid_attention_grads/pallas_call | solution.py:100
  73.4 30.6 %all_to_all.16 = bf16[64,16,896]{2,1,0:T(8,128)(2,1)S(1)} all-to-all(bf16[64,16,896]{2,1,0:T(8,128)(2,1)S(1)} %grid_attention_grads.1), channel_id=1, replica_groups=mesh['zl'=2,'x'=4,'y'=4,'zh'=2,'core'=2] {'zl','x','y','zh'}, dimensions={0} | all-to-all | bytes 3670016 | tf_op jit(solution)/shard_map/all_to_all | solution.py:146
  104.0 0.1 convert_reduce_fusion
  104.2 0.1 collective-permute-start
  104.2 1.2 collective-permute-done
  105.4 0.9 broadcast_in_dim.2
  106.4 5.5 %all-to-all-start.2 = ((bf16[64,16,384]{2,1,0:T(8,128)(2,1)}), bf16[64,16,384]{2,1,0:T(8,128)(2,1)}, u32[]{:S(2)}, u32[]{:S(2)}) async-start(bf16[64,16,384]{2,1,0:T(8,128)(2,1)} %broadcast_in_dim.2), calls=%async_computation.2 | async-start | bytes 1572864 | tf_op jit(solution)/shard_map/all_to_all | solution.py:150
  111.9 0.1 slice.8
  112.0 0.3 reshape.39
  112.3 1.2 copy.11
  113.5 14.8 %all-to-all-done.2.y = bf16[64,16,384]{2,1,0:T(8,128)(2,1)} async-done(((bf16[64,16,384]{2,1,0:T(8,128)(2,1)}), bf16[64,16,384]{2,1,0:T(8,128)(2,1)}, u32[]{:S(2)}, u32[]{:S(2)}) %all-to-all-start.2) | async-done | bytes 786464 | tf_op jit(solution)/shard_map/all_to_all | solution.py:150
  128.2 2.2 %parameter_grads.1 = (f32[256,768]{1,0:T(8,128)}, f32[256,256]{1,0:T(8,128)}, f32[512,64]{1,0:T(8,128)}, f32[1,256]{1,0:T(1,128)}) custom-call(bf16[64,16,384]{2,1,0:T(8,128)(2,1)} %all-to-all-done.2.y), custom_call_target="tpu_custom_call" | custom-call | tf_op jit(solution)/shard_map/parameter_grads/pallas_call | solution.py:123
  (1 shorter events, 0.0 us)
Async XLA Ops:
  2.3 41.2 %copy-start = (bf16[256,768]{1,0:T(8,128)(2,1)S(1)}, bf16[256,768]{1,0:T(8,128)(2,1)}, u32[]{:S(2)}) copy-start(bf16[256,768]{1,0:T(8,128)(2,1)} %wqkv.1) | copy-start | bytes 1179652
  2.4 41.2 %copy-start.1 = (f32[8,64,64]{2,1,0:T(8,128)S(1)}, f32[8,64,64]{2,1,0:T(8,128)}, u32[]{:S(2)}) copy-start(f32[8,64,64]{2,1,0:T(8,128)} %param.11) | copy-start | bytes 393220
  2.4 41.2 %copy-start.2 = (bf16[256,256]{1,0:T(8,128)(2,1)S(1)}, bf16[256,256]{1,0:T(8,128)(2,1)}, u32[]{:S(2)}) copy-start(bf16[256,256]{1,0:T(8,128)(2,1)} %wout.1) | copy-start | bytes 393220
  2.4 41.2 %copy-start.3 = (f32[256]{0:T(256)S(1)}, f32[256]{0:T(256)}, u32[]{:S(2)}) copy-start(f32[256]{0:T(256)} %param.8) | copy-start | bytes 3076
  104.2 1.3 collective-permute-start
  106.4 21.9 %all-to-all-start.2 = ((bf16[64,16,384]{2,1,0:T(8,128)(2,1)}), bf16[64,16,384]{2,1,0:T(8,128)(2,1)}, u32[]{:S(2)}, u32[]{:S(2)}) async-start(bf16[64,16,384]{2,1,0:T(8,128)(2,1)} %broadcast_in_dim.2), calls=%async_computation.2 | async-start | bytes 1572864 | tf_op jit(solution)/shard_map/all_to_all | solution.py:150
where the time goes:
time: 131 us; the launch traced here: 130 us
  blocking collectives  71.8 us (55%)
  Pallas kernels  32 us (24%)
  waiting for transfers between devices  15.9 us (12%)
  starting transfers between devices  5.55 us (4%)
  local copies, waits for them, and re-layouts  2.58 us (2%)
  other arithmetic  1.85 us (1%)
    all_to_all x1, blocking collectives, on_device(): arrived = lax.all_to_all(both, CHIPS, 0, 0, tiled=True)  41.2 us
    all_to_all x1, blocking collectives, on_device(): returned = lax.all_to_all(message, CHIPS, 0, 0, tiled=True)  30.6 us
    pallas_call x1, Pallas kernels, layer(): pl.pallas_call(functools.partial(layer_kernel, NB), out_shape=jax.ShapeDt...  29.8 us
    all_to_all x1, waiting for transfers between devices, on_device(): totals = lax.all_to_all(total, CHIPS, 0, 0, tiled=True)  14.8 us
    all_to_all x1, starting transfers between devices, on_device(): totals = lax.all_to_all(total, CHIPS, 0, 0, tiled=True)  5.47 us
  transfers between devices with their start and end apart: 2, of which 2 were waited for; matrix products, arithmetic and copies ran while one was open for 1% of the time, Pallas kernels for 0%

commit v1 on v0

v1 whole, which is shorter than its diff:
```python
import functools, math
import jax, jax.numpy as jnp
from jax import lax
from jax.experimental import pallas as pl
from jax.experimental.pallas import tpu as pltpu
from jax.sharding import PartitionSpec as P
F32=jnp.float32; BF=jnp.bfloat16
SC=32**-0.5; L2E=math.log2(math.e)
NT=(((1,),(1,)),((),())); TN=(((0,),(0,)),((),())); NN=(((1,),(0,)),((),()))
ST=40
def dg(a,b,d): return lax.dot_general(a,b,d,preferred_element_type=F32)
def attention(NB,Q,K,V,dA,biasT,expand,pick):
    units=[(k,hf) for k in range(NB) for hf in range(2)]
    def sl(a,k,hf): return a[64*k:64*k+64,128*hf:128*hf+128]
    qx={};dax={};t={};dp={};pb={};sb={};o={}
    db=[None]*2
    ch=2*NB
    for c0 in range(0,len(units),ch):
        us=units[c0:c0+ch]
        for u in us:
            qx[u]=expand(sl(Q,*u)); dax[u]=expand(sl(dA,*u))
            t[u]=dg(sl(K,*u),qx[u],NT); dp[u]=dg(sl(V,*u),dax[u],NT)
        for u in us:
            hf=u[1]
            x=t[u]+biasT[:,256*hf:256*hf+256]
            m=jnp.max(x,0,keepdims=True)
            e=jnp.exp2(x-m)
            p=e*(1.0/jnp.sum(e,0,keepdims=True))
            pb[u]=p.astype(BF)
            D=jnp.sum(dp[u]*p,0,keepdims=True)
            s=p*(dp[u]-D)
            sb[u]=s.astype(BF)
            db[hf]=s if db[hf] is None else db[hf]+s
        for u in us:
            o[u]=(pick(dg(pb[u],sl(V,*u),TN)).astype(BF),dg(pb[u],dax[u],NN).astype(BF),
                  (dg(sb[u],qx[u],NN)*(1.0/L2E)).astype(BF),(pick(dg(sb[u],sl(K,*u),TN))*SC).astype(BF))
    return o,db
def layer_kernel(NB,recv,gain,wqkv,wout,bias,msg,xf0,xf1,dyf0,dyf1,biasT,dbias,ggain,nrm,inv_s,nS,qS,kS,vS,daS,dS,aS,gS):
    def cvt(s,_):
        t=recv[s]
        for i,ref in enumerate((xf0,xf1,dyf0,dyf1)):
            ref[pl.ds(s*ST,32),:]=t[:,128*i:128*i+128].astype(F32)
        return 0
    lax.fori_loop(0,64,cvt,0,unroll=8)
    for q in range(4):
        biasT[:,128*q:128*(q+1)]=(bias[128*q:128*(q+1),:]*L2E).T
    dbias[...]=jnp.zeros_like(dbias); ggain[...]=jnp.zeros_like(ggain)
    lane=lax.broadcasted_iota(jnp.int32,(64,128),1)//32
    masks=[lane==h for h in range(4)]
    zero=jnp.zeros((64,128),BF)
    def expand(a):
        return jnp.concatenate([jnp.where(m,a,zero) for m in masks],axis=0)
    def pick(r):
        o=r[0:64]
        for h in range(1,4): o=jnp.where(masks[h],r[64*h:64*h+64],o)
        return o
    w=wqkv[...]; wo=wout[...]; gn=gain[...]
    PA=8; RA=64*PA
    def phase_a(b,_):
        def grouped(lo,hi):
            return jnp.concatenate([jnp.concatenate([ref[pl.ds(b*PA+k,64,stride=ST),:] for k in range(PA)],0) for ref in (lo,hi)],1)
        rr=pl.ds(pl.multiple_of(b*RA,RA),RA)
        x=grouped(xf0,xf1); dyb=grouped(dyf0,dyf1).astype(BF)
        dS[rr,:]=dyb
        daS[rr,:]=dg(dyb,wo,NT).astype(BF)
        c=x-jnp.mean(x,-1,keepdims=True)
        inv=lax.rsqrt(jnp.mean(c*c,-1,keepdims=True)+1e-5)
        normal=c*inv
        nrm[rr,:]=normal; inv_s[rr,:]=jnp.broadcast_to(inv,(RA,128))
        normed=(normal*gn).astype(BF)
        nS[rr,:]=normed
        packed=dg(normed,w,NN)
        qS[rr,:]=(packed[:,:256]*(SC*L2E)).astype(BF); kS[rr,:]=packed[:,256:512].astype(BF); vS[rr,:]=packed[:,512:].astype(BF)
        return 0
    lax.fori_loop(0,32//PA,phase_a,0,unroll=4)
    RB=64*NB
    def phase_b(b,_):
        rr=pl.ds(pl.multiple_of(b*RB,RB),RB)
        o,db=attention(NB,qS[rr,:],kS[rr,:],vS[rr,:],daS[rr,:],biasT,expand,pick)
        for k in range(NB):
            r=pl.ds(pl.multiple_of(b*RB+64*k,64),64)
            for hf in range(2):
                a,gv,gk,gq=o[(k,hf)]
                l=slice(128*hf,128*hf+128)
                aS[r,l]=a
                gS[r,128*hf:128*hf+128]=gq; gS[r,256+128*hf:384+128*hf]=gk; gS[r,512+128*hf:640+128*hf]=gv
        for hf in range(2): dbias[:,256*hf:256*hf+256]+=db[hf]
        return 0
    lax.fori_loop(0,32//NB,phase_b,0,unroll=1)
    PC=8; RC=64*PC
    def phase_c(b,_):
        rr=pl.ds(pl.multiple_of(b*RC,RC),RC)
        gN=dg(gS[rr,:],w,NT)
        normal=nrm[rr,:]
        i1=inv_s[rr,:]; inv=jnp.concatenate([i1,i1],1)
        gx=gN*normal
        ggain[...]+=jnp.sum(gx.reshape(-1,8,256),0)
        g=gN*gn
        dx=dS[rr,:].astype(F32)+inv*(g-jnp.mean(g,-1,keepdims=True)-normal*jnp.mean(gx*gn,-1,keepdims=True))
        for k in range(PC):
            xf0[pl.ds(b*PC+k,64,stride=ST),:]=dx[64*k:64*k+64,:128]
            xf1[pl.ds(b*PC+k,64,stride=ST),:]=dx[64*k:64*k+64,128:]
        return 0
    lax.fori_loop(0,32//PC,phase_c,0,unroll=4)
    gqkv=dg(nS[...],gS[...],TN).astype(BF)
    gproj=dg(aS[...],dS[...],TN).astype(BF)
    for rb in range(16):
        rr=slice(16*rb,16*rb+16)
        msg[rb*3,:,512:896]=gqkv[rr,0:384]
        msg[rb*3+1,:,512:896]=gqkv[rr,384:768]
        msg[rb*3+2,:,512:768]=gproj[rr,:]
        q=rb//4; j0=16*(rb%4)
        msg[rb*3+2,:,768:896]=dbias[j0:j0+16,128*q:128*q+128].astype(BF)
    def wr(s,_):
        for i,ref in enumerate((xf0,xf1)):
            t=ref[pl.ds(s*ST,32),:].astype(BF)
            msg[s,:,128*i:128*i+128]=t[:16]
            msg[s,:,256+128*i:384+128*i]=t[16:]
        return 0
    lax.fori_loop(0,64,wr,0,unroll=8)
    msg[48:64,:,512:896]=jnp.zeros((16,16,384),BF)
    gs=jnp.sum(ggain[...],0,keepdims=True)
    msg[48,:,512:768]=jnp.broadcast_to(gs,(16,256)).astype(BF)
def layer(recv,gain,wqkv,wout,bias,NB=8):
    vm=pl.BlockSpec(memory_space=pltpu.VMEM)
    return pl.pallas_call(functools.partial(layer_kernel,NB),
        out_shape=jax.ShapeDtypeStruct((64,16,896),BF),
        in_specs=[vm]*5,out_specs=vm,
        scratch_shapes=[*[pltpu.VMEM((64*ST,128),F32)]*4,pltpu.VMEM((64,512),F32),pltpu.VMEM((64,512),F32),pltpu.VMEM((8,256),F32),
            pltpu.VMEM((2048,256),F32),pltpu.VMEM((2048,128),F32),*[pltpu.VMEM((2048,256),BF)]*7,pltpu.VMEM((2048,768),BF)],
        compiler_params=pltpu.CompilerParams(vmem_limit_bytes=48*2**20),
        name="grid_attention_grads")(recv,gain.reshape(1,256),wqkv,wout,bias.reshape(512,64))


def finish_kernel(y, qkv, proj, bias, gain):
    for rb in range(16):
        rr = slice(16 * rb, 16 * rb + 16)
        qkv[rr, 0:384] = y[rb * 3].astype(F32)
        qkv[rr, 384:768] = y[rb * 3 + 1].astype(F32)
        proj[rr, :] = y[rb * 3 + 2, :, 0:256].astype(F32)
    for q in range(4):
        t = jnp.concatenate([y[(q * 4 + r) * 3 + 2, :, 256:384].astype(F32) for r in range(4)], 0)
        bias[128 * q : 128 * q + 128, :] = t.T
    gain[...] = y[48, 0:1, 0:256].astype(F32)


def finish(y):
    vm = pl.BlockSpec(memory_space=pltpu.VMEM)
    return pl.pallas_call(
        finish_kernel,
        out_shape=(
            jax.ShapeDtypeStruct((256, 768), F32),
            jax.ShapeDtypeStruct((256, 256), F32),
            jax.ShapeDtypeStruct((512, 64), F32),
            jax.ShapeDtypeStruct((1, 256), F32),
        ),
        in_specs=[vm],
        out_specs=(vm,) * 4,
        name="parameter_grads",
    )(y)


CHIPS = ("zl", "x", "y", "zh")


def on_device(activations, cotangent, ln_gain, qkv_weight, out_weight, position_bias):
    both = jnp.concatenate(
        [activations.reshape(64, 32, 256), cotangent.reshape(64, 32, 256)], axis=2
    )
    arrived = lax.all_to_all(both, CHIPS, 0, 0, tiled=True)
    message = layer(arrived, ln_gain, qkv_weight, out_weight, position_bias)
    returned = lax.all_to_all(message, CHIPS, 0, 0, tiled=True)
    partial = jnp.sum(returned[:, :, 512:].astype(F32), axis=0)
    other = lax.ppermute(partial, "core", [(0, 1), (1, 0)])
    total = jnp.broadcast_to((partial + other).astype(BF)[None], (64, 16, 384))
    totals = lax.all_to_all(total, CHIPS, 0, 0, tiled=True)
    grad_input = returned[:, :, :512].reshape(64, 16, 2, 256).transpose(0, 2, 1, 3)
    grad_input = grad_input.reshape(activations.shape)
    grad_qkv, grad_proj, grad_bias, grad_gain = finish(totals)
    return (
        grad_input,
        grad_gain.reshape(256),
        grad_qkv,
        grad_proj,
        grad_bias.reshape(8, 64, 64),
    )


def solution(mesh):
    fine = jax.sharding.Mesh(mesh.devices.reshape(2, 4, 4, 2, 2), ("zl", "x", "y", "zh", "core"))
    tokens = P(None, ("zl", "x"), ("y", "zh", "core"), None)
    return jax.shard_map(
        on_device,
        mesh=fine,
        in_specs=(tokens, tokens, P(), P(), P(), P()),
        out_specs=(tokens, P(), P(), P(), P()),
        check_vma=False,
    )
```

time: 131 us -> 114 us (0.87)
  Pallas kernels: 32 us -> 15.3 us
    pallas_call x1, Pallas kernels: 29.8 us -> 13.1 us  [layer(): pl.pallas_call(functools.partial(layer_kernel, NB), out_shape=jax.ShapeDt...]
where the time goes in v1:
time: 114 us
  blocking collectives  71.8 us (63%)
  waiting for transfers between devices  15.9 us (14%)
  Pallas kernels  15.3 us (13%)
  starting transfers between devices  5.55 us (5%)
  local copies, waits for them, and re-layouts  2.58 us (2%)
  other arithmetic  1.85 us (2%)
    all_to_all x1, blocking collectives, on_device(): arrived = lax.all_to_all(both, CHIPS, 0, 0, tiled=True)  41.2 us
    all_to_all x1, blocking collectives, on_device(): returned = lax.all_to_all(message, CHIPS, 0, 0, tiled=True)  30.6 us
    all_to_all x1, waiting for transfers between devices, on_device(): totals = lax.all_to_all(total, CHIPS, 0, 0, tiled=True)  14.8 us
    pallas_call x1, Pallas kernels, layer(): pl.pallas_call(functools.partial(layer_kernel, NB), out_shape=jax.ShapeDt...  13.1 us
    all_to_all x1, starting transfers between devices, on_device(): totals = lax.all_to_all(total, CHIPS, 0, 0, tiled=True)  5.47 us
  transfers between devices with their start and end apart: 2, of which 2 were waited for; matrix products, arithmetic and copies ran while one was open for 1% of the time, Pallas kernels for 0%

profile of v1, /device:TPU:0, one launch (start us, length us, event | category | flops | bytes accessed | tf_op | source)
XLA Modules:
  0.0 113.7 jit_solution(4459863510148029066)
XLA Ops:
  0.6 1.7 %pad_maximum_fusion = bf16[64,32,512]{2,1,0:T(8,128)(2,1)S(1)} fusion(bf16[64,32,256]{2,1,0:T(8,128)(2,1)} %bitcast.12, bf16[64,32,256]{2,1,0:T(8,128)(2,1)} %bitcast.13), kind=kLoop, calls=%fused_computation | loop fusion | flops 4194304 | bytes 4194304 | tf_op jit(solution)/shard_map/concatenate | solution.py:167
  2.3 0.0 copy-start
  2.4 0.0 copy-start.1
  2.4 0.0 copy-start.2
  2.4 0.0 copy-start.3
  2.4 41.2 %all_to_all.15.recv = bf16[64,32,512]{2,1,0:T(8,128)(2,1)S(1)} all-to-all(bf16[64,32,512]{2,1,0:T(8,128)(2,1)S(1)} %pad_maximum_fusion), channel_id=1, replica_groups=mesh['zl'=2,'x'=4,'y'=4,'zh'=2,'core'=2] {'zl','x','y','zh'}, dimensions={0} | all-to-all | bytes 4194304 | tf_op jit(solution)/shard_map/all_to_all | solution.py:170
  43.5 0.0 copy-done
  43.5 0.0 copy-done.1
  43.5 0.0 copy-done.2
  43.6 0.0 copy-done.3
  43.6 13.1 %grid_attention_grads.1 = bf16[64,16,896]{2,1,0:T(8,128)(2,1)S(1)} custom-call(bf16[64,32,512]{2,1,0:T(8,128)(2,1)S(1)} %all_to_all.15.recv, f32[1,256]{1,0:T(1,128)S(1)} %bitcast.9, bf16[256,768]{1,0:T(8,128)(2,1)S(1)} %copy-done, bf16[256,256]{1,0:T(8,128)(2,1)S(1)} %copy-done.2, f32[512,64]{1,0:T(8,128)S(1)} %bitcast.8), custom_call_target="tpu_custom_call" | custom-call | tf_op jit(solution)/shard_map/grid_attention_grads/pallas_call | solution.py:126
  56.6 30.6 %all_to_all.16 = bf16[64,16,896]{2,1,0:T(8,128)(2,1)S(1)} all-to-all(bf16[64,16,896]{2,1,0:T(8,128)(2,1)S(1)} %grid_attention_grads.1), channel_id=1, replica_groups=mesh['zl'=2,'x'=4,'y'=4,'zh'=2,'core'=2] {'zl','x','y','zh'}, dimensions={0} | all-to-all | bytes 3670016 | tf_op jit(solution)/shard_map/all_to_all | solution.py:172
  87.3 0.1 convert_reduce_fusion
  87.4 0.1 collective-permute-start
  87.5 1.2 %collective-permute-done = f32[16,384]{1,0:T(8,128)S(1)} collective-permute-done((f32[16,384]{1,0:T(8,128)S(1)}, f32[16,384]{1,0:T(8,128)S(1)}, u32[]{:S(2)}, u32[]{:S(2)}) %collective-permute-start) | collective-permute-done | bytes 24608 | tf_op jit(solution)/shard_map/ppermute | solution.py:174
  88.7 0.9 broadcast_in_dim.2
  89.6 5.5 %all-to-all-start.2 = ((bf16[64,16,384]{2,1,0:T(8,128)(2,1)}), bf16[64,16,384]{2,1,0:T(8,128)(2,1)}, u32[]{:S(2)}, u32[]{:S(2)}) async-start(bf16[64,16,384]{2,1,0:T(8,128)(2,1)} %broadcast_in_dim.2), calls=%async_computation.2 | async-start | bytes 1572864 | tf_op jit(solution)/shard_map/all_to_all | solution.py:176
  95.1 0.1 slice.8
  95.3 0.3 reshape.39
  95.6 1.2 %copy.11 = bf16[64,2,16,256]{3,2,1,0:T(8,128)(2,1)} copy(bf16[64,2,16,256]{3,1,2,0:T(2,128)(2,1)S(1)} %bitcast.10) | data formatting | bytes 2097152 | tf_op jit(solution)/shard_map/transpose | solution.py:177
  96.7 14.8 %all-to-all-done.2.y = bf16[64,16,384]{2,1,0:T(8,128)(2,1)} async-done(((bf16[64,16,384]{2,1,0:T(8,128)(2,1)}), bf16[64,16,384]{2,1,0:T(8,128)(2,1)}, u32[]{:S(2)}, u32[]{:S(2)}) %all-to-all-start.2) | async-done | bytes 786464 | tf_op jit(solution)/shard_map/all_to_all | solution.py:176
  111.5 2.2 %parameter_grads.1 = (f32[256,768]{1,0:T(8,128)}, f32[256,256]{1,0:T(8,128)}, f32[512,64]{1,0:T(8,128)}, f32[1,256]{1,0:T(1,128)}) custom-call(bf16[64,16,384]{2,1,0:T(8,128)(2,1)} %all-to-all-done.2.y), custom_call_target="tpu_custom_call" | custom-call | tf_op jit(solution)/shard_map/parameter_grads/pallas_call | solution.py:149
  (1 shorter events, 0.0 us)
Async XLA Ops:
  2.3 41.2 %copy-start = (bf16[256,768]{1,0:T(8,128)(2,1)S(1)}, bf16[256,768]{1,0:T(8,128)(2,1)}, u32[]{:S(2)}) copy-start(bf16[256,768]{1,0:T(8,128)(2,1)} %wqkv.1) | copy-start | bytes 1179652
  2.4 41.2 %copy-start.1 = (f32[8,64,64]{2,1,0:T(8,128)S(1)}, f32[8,64,64]{2,1,0:T(8,128)}, u32[]{:S(2)}) copy-start(f32[8,64,64]{2,1,0:T(8,128)} %param.11) | copy-start | bytes 393220
  2.4 41.2 %copy-start.2 = (bf16[256,256]{1,0:T(8,128)(2,1)S(1)}, bf16[256,256]{1,0:T(8,128)(2,1)}, u32[]{:S(2)}) copy-start(bf16[256,256]{1,0:T(8,128)(2,1)} %wout.1) | copy-start | bytes 393220
  2.4 41.2 %copy-start.3 = (f32[256]{0:T(256)S(1)}, f32[256]{0:T(256)}, u32[]{:S(2)}) copy-start(f32[256]{0:T(256)} %param.8) | copy-start | bytes 3076
  87.4 1.3 %collective-permute-start = (f32[16,384]{1,0:T(8,128)S(1)}, f32[16,384]{1,0:T(8,128)S(1)}, u32[]{:S(2)}, u32[]{:S(2)}) collective-permute-start(f32[16,384]{1,0:T(8,128)S(1)} %convert_reduce_fusion), channel_id=1, source_target_pairs={{0,1},{1,0},{2,3},{3,2},{4,5},{5,4},{6,7},{7,6},{8,9},{9,8},{10,11... | collective-permute-start | bytes 73736 | tf_op jit(solution)/shard_map/ppermute | solution.py:174
  89.6 21.9 %all-to-all-start.2 = ((bf16[64,16,384]{2,1,0:T(8,128)(2,1)}), bf16[64,16,384]{2,1,0:T(8,128)(2,1)}, u32[]{:S(2)}, u32[]{:S(2)}) async-start(bf16[64,16,384]{2,1,0:T(8,128)(2,1)} %broadcast_in_dim.2), calls=%async_computation.2 | async-start | bytes 1572864 | tf_op jit(solution)/shard_map/all_to_all | solution.py:176

commit v2 on v0

v2 whole, which is shorter than its diff:
```python
import functools
import math

import jax
import jax.numpy as jnp
from jax import lax
from jax.experimental import pallas as pl
from jax.experimental.pallas import tpu as pltpu
from jax.sharding import PartitionSpec as P

F32 = jnp.float32
BF = jnp.bfloat16
MEMBERS = 64
GROUPS = 32
TOKENS = MEMBERS * GROUPS
STRIDE = 40
SCALE = 32**-0.5
LOG2E = math.log2(math.e)
NN = (((1,), (0,)), ((), ()))
NT = (((1,), (1,)), ((), ()))
TN = (((0,), (0,)), ((), ()))
CHIPS = ("zl", "x", "y", "zh")
VM = pl.BlockSpec(memory_space=pltpu.VMEM)
HBM = pl.BlockSpec(memory_space=pltpu.HBM)
MIB = 2**20


def dot(a, b, dims):
    return lax.dot_general(a, b, dims, preferred_element_type=F32)


def unpack(recv, refs):
    def step(s, _):
        rows = recv[s]
        for i, ref in enumerate(refs):
            ref[pl.ds(s * STRIDE, GROUPS), :] = rows[:, 128 * i : 128 * i + 128].astype(F32)
        return 0

    lax.fori_loop(0, MEMBERS, step, 0, unroll=8)


def grouped(refs, first, count):
    columns = [
        jnp.concatenate(
            [ref[pl.ds(first + k, MEMBERS, stride=STRIDE), :] for k in range(count)], axis=0
        )
        for ref in refs
    ]
    return jnp.concatenate(columns, axis=1)


def normalise(x):
    centred = x - jnp.mean(x, -1, keepdims=True)
    inverse = lax.rsqrt(jnp.mean(centred * centred, -1, keepdims=True) + 1e-5)
    return centred * inverse, inverse


def head_masks():
    lane = lax.broadcasted_iota(jnp.int32, (MEMBERS, 128), 1) // 32
    return [lane == h for h in range(4)]


def expand(a, masks):
    zero = jnp.zeros_like(a)
    return jnp.concatenate([jnp.where(m, a, zero) for m in masks], axis=0)


def pick(r, masks):
    out = r[0:MEMBERS]
    for h in range(1, 4):
        out = jnp.where(masks[h], r[MEMBERS * h : MEMBERS * (h + 1)], out)
    return out


def attention(count, q, k, v, da, bias, masks):
    units = [(g, hf) for g in range(count) for hf in range(2)]

    def part(a, u):
        g, hf = u
        return a[MEMBERS * g : MEMBERS * (g + 1), 128 * hf : 128 * (hf + 1)]

    qx = {u: expand(part(q, u), masks) for u in units}
    dax = {u: expand(part(da, u), masks) for u in units}
    scores = {}
    grad_probs = {}
    for u in units:
        scores[u] = dot(part(k, u), qx[u], NT)
        grad_probs[u] = dot(part(v, u), dax[u], NT)
    weights = {}
    scaled = {}
    grad_bias = [None, None]
    for u in units:
        hf = u[1]
        logits = scores[u] + bias[:, 256 * hf : 256 * (hf + 1)]
        e = jnp.exp2(logits - jnp.max(logits, 0, keepdims=True))
        p = e * (1.0 / jnp.sum(e, 0, keepdims=True))
        ds = p * (grad_probs[u] - jnp.sum(grad_probs[u] * p, 0, keepdims=True))
        weights[u] = p.astype(BF)
        scaled[u] = ds.astype(BF)
        grad_bias[hf] = ds if grad_bias[hf] is None else grad_bias[hf] + ds
    results = {}
    for u in units:
        attended = pick(dot(weights[u], part(v, u), TN), masks)
        grad_v = dot(weights[u], dax[u], NN)
        grad_k = dot(scaled[u], qx[u], NN) * (1.0 / LOG2E)
        grad_q = pick(dot(scaled[u], part(k, u), TN), masks) * SCALE
        results[u] = [r.astype(BF) for r in (attended, grad_q, grad_k, grad_v)]
    return results, grad_bias


def gradients_kernel(
    recv, gain, wqkv, wout, bias, msg, grad_packed,
    x0, x1, d0, d1, bias_t, grad_bias, normed_s, q_s, k_s, v_s, da_s, dy_s, att_s, gp_s, sem,
):
    unpack(recv, (x0, x1, d0, d1))
    for t in range(4):
        bias_t[:, 128 * t : 128 * (t + 1)] = (bias[128 * t : 128 * (t + 1), :] * LOG2E).T
    grad_bias[...] = jnp.zeros_like(grad_bias)
    masks = head_masks()

    def project(b, _):
        rows = pl.ds(pl.multiple_of(b * 512, 512), 512)
        dy = grouped((d0, d1), b * 8, 8).astype(BF)
        dy_s[rows, :] = dy
        da_s[rows, :] = dot(dy, wout[...], NT).astype(BF)
        normal, _ = normalise(grouped((x0, x1), b * 8, 8))
        normed = (normal * gain[...]).astype(BF)
        normed_s[rows, :] = normed
        packed = dot(normed, wqkv[...], NN)
        q_s[rows, :] = (packed[:, :256] * (SCALE * LOG2E)).astype(BF)
        k_s[rows, :] = packed[:, 256:512].astype(BF)
        v_s[rows, :] = packed[:, 512:].astype(BF)
        return 0

    lax.fori_loop(0, GROUPS // 8, project, 0, unroll=4)

    def attend(b, _):
        rows = pl.ds(pl.multiple_of(b * 512, 512), 512)
        results, gb = attention(
            8, q_s[rows, :], k_s[rows, :], v_s[rows, :], da_s[rows, :], bias_t, masks
        )
        for (g, hf), (att, gq, gk, gv) in results.items():
            r = pl.ds(pl.multiple_of(b * 512 + MEMBERS * g, MEMBERS), MEMBERS)
            att_s[r, 128 * hf : 128 * (hf + 1)] = att
            for i, part in enumerate((gq, gk, gv)):
                gp_s[r, 256 * i + 128 * hf : 256 * i + 128 * (hf + 1)] = part
        for hf in range(2):
            grad_bias[:, 256 * hf : 256 * (hf + 1)] += gb[hf]
        return 0

    lax.fori_loop(0, GROUPS // 8, attend, 0)
    copy = pltpu.make_async_copy(gp_s, grad_packed, sem)
    copy.start()
    grad_qkv = dot(normed_s[...], gp_s[...], TN).astype(BF)
    grad_proj = dot(att_s[...], dy_s[...], TN).astype(BF)
    for rb in range(16):
        rr = slice(16 * rb, 16 * rb + 16)
        t, j = rb // 4, 16 * (rb % 4)
        msg[3 * rb] = grad_qkv[rr, 0:384]
        msg[3 * rb + 1] = grad_qkv[rr, 384:768]
        msg[3 * rb + 2, :, 0:256] = grad_proj[rr, :]
        msg[3 * rb + 2, :, 256:384] = grad_bias[j : j + 16, 128 * t : 128 * (t + 1)].astype(BF)
    msg[48:64] = jnp.zeros((16, 16, 384), BF)
    copy.wait()


def gradients(recv, gain, wqkv, wout, bias):
    return pl.pallas_call(
        gradients_kernel,
        out_shape=(
            jax.ShapeDtypeStruct((64, 16, 384), BF),
            jax.ShapeDtypeStruct((TOKENS, 768), BF),
        ),
        in_specs=[VM] * 5,
        out_specs=(VM, HBM),
        scratch_shapes=[
            *[pltpu.VMEM((MEMBERS * STRIDE, 128), F32)] * 4,
            *[pltpu.VMEM((MEMBERS, 512), F32)] * 2,
            *[pltpu.VMEM((TOKENS, 256), BF)] * 7,
            pltpu.VMEM((TOKENS, 768), BF),
            pltpu.SemaphoreType.DMA,
        ],
        compiler_params=pltpu.CompilerParams(vmem_limit_bytes=50 * MIB),
        cost_estimate=pl.CostEstimate(
            flops=8 * 10**9, bytes_accessed=8 * 2**20, transcendentals=8 * 2**20
        ),
        name="parameter_gradients",
    )(recv, gain, wqkv, wout, bias)


def input_kernel(recv, grad_packed, gain, wqkv, out, x0, x1, d0, d1, gp_s, sem):
    copy = pltpu.make_async_copy(grad_packed, gp_s, sem)
    copy.start()
    unpack(recv, (x0, x1, d0, d1))
    copy.wait()

    def block(b, _):
        rows = pl.ds(pl.multiple_of(b * 512, 512), 512)
        g = dot(gp_s[rows, :], wqkv[...], NT) * gain[...]
        normal, inverse = normalise(grouped((x0, x1), b * 8, 8))
        along = jnp.mean(g * normal, -1, keepdims=True)
        dx = inverse * (g - jnp.mean(g, -1, keepdims=True) - normal * along)
        dx = grouped((d0, d1), b * 8, 8) + dx
        for k in range(8):
            for i, ref in enumerate((x0, x1)):
                ref[pl.ds(b * 8 + k, MEMBERS, stride=STRIDE), :] = dx[
                    MEMBERS * k : MEMBERS * (k + 1), 128 * i : 128 * (i + 1)
                ]
        return 0

    lax.fori_loop(0, GROUPS // 8, block, 0, unroll=4)

    def write(s, _):
        for i, ref in enumerate((x0, x1)):
            rows = ref[pl.ds(s * STRIDE, GROUPS), :].astype(BF)
            out[s, :, 128 * i : 128 * i + 128] = rows[:16]
            out[s, :, 256 + 128 * i : 384 + 128 * i] = rows[16:]
        return 0

    lax.fori_loop(0, MEMBERS, write, 0, unroll=8)


def input_gradient(recv, grad_packed, gain, wqkv):
    return pl.pallas_call(
        input_kernel,
        out_shape=jax.ShapeDtypeStruct((64, 16, 512), BF),
        in_specs=[VM, HBM, VM, VM],
        out_specs=VM,
        scratch_shapes=[
            *[pltpu.VMEM((MEMBERS * STRIDE, 128), F32)] * 4,
            pltpu.VMEM((TOKENS, 768), BF),
            pltpu.SemaphoreType.DMA,
        ],
        compiler_params=pltpu.CompilerParams(vmem_limit_bytes=50 * MIB),
        cost_estimate=pl.CostEstimate(
            flops=6 * 10**9, bytes_accessed=16 * 2**20, transcendentals=2**20
        ),
        name="input_gradient",
    )(recv, grad_packed, gain, wqkv)


def spread_kernel(mine, other, dx, out):
    total = (mine[...] + other[...]).astype(BF)

    def step(d, _):
        out[d, :, 0:512] = dx[d]
        out[d, :, 512:896] = total
        return 0

    lax.fori_loop(0, 64, step, 0, unroll=8)


def spread(mine, other, dx):
    return pl.pallas_call(
        spread_kernel,
        out_shape=jax.ShapeDtypeStruct((64, 16, 896), BF),
        in_specs=[VM] * 3,
        out_specs=VM,
        compiler_params=pltpu.CompilerParams(vmem_limit_bytes=8 * MIB),
        name="spread_sums",
    )(mine, other, dx)


def finish_kernel(y, gain, wqkv, dx, qkv, proj, bias, ggain, weight, sem):
    copy = pltpu.make_async_copy(wqkv, weight, sem)
    copy.start()

    def step(s, _):
        dx[s, 0:16, :] = y[s, :, 0:256]
        dx[s, 16:32, :] = y[s, :, 256:512]
        return 0

    lax.fori_loop(0, 64, step, 0, unroll=8)
    for rb in range(16):
        rr = slice(16 * rb, 16 * rb + 16)
        qkv[rr, 0:384] = y[3 * rb, :, 512:896].astype(F32)
        qkv[rr, 384:768] = y[3 * rb + 1, :, 512:896].astype(F32)
        proj[rr, :] = y[3 * rb + 2, :, 512:768].astype(F32)
    for t in range(4):
        tile = [y[(t * 4 + r) * 3 + 2, :, 768:896].astype(F32) for r in range(4)]
        bias[128 * t : 128 * (t + 1), :] = jnp.concatenate(tile, 0).T
    copy.wait()
    along = jnp.sum(qkv[...] * weight[...].astype(F32), -1, keepdims=True)
    ggain[...] = jnp.broadcast_to(along, (256, 128)).T[0:1] / gain[...]


def finish(y, gain, wqkv):
    return pl.pallas_call(
        finish_kernel,
        out_shape=(
            jax.ShapeDtypeStruct((64, 32, 256), BF),
            jax.ShapeDtypeStruct((256, 768), F32),
            jax.ShapeDtypeStruct((256, 256), F32),
            jax.ShapeDtypeStruct((512, 64), F32),
            jax.ShapeDtypeStruct((1, 256), F32),
        ),
        in_specs=[VM, VM, HBM],
        out_specs=(VM,) * 5,
        scratch_shapes=[pltpu.VMEM((256, 768), BF), pltpu.SemaphoreType.DMA],
        compiler_params=pltpu.CompilerParams(vmem_limit_bytes=12 * MIB),
        name="place_results",
    )(y, gain, wqkv)


def on_device(activations, cotangent, ln_gain, qkv_weight, out_weight, position_bias):
    both = jnp.concatenate(
        [activations.reshape(64, 32, 256), cotangent.reshape(64, 32, 256)], axis=2
    )
    arrived = lax.all_to_all(both, CHIPS, 0, 0, tiled=True)
    gain = ln_gain.reshape(1, 256)
    partials, grad_packed = gradients(
        arrived, gain, qkv_weight, out_weight, position_bias.reshape(512, 64)
    )
    shares = lax.all_to_all(partials, CHIPS, 0, 0, tiled=True)
    message = input_gradient(arrived, grad_packed, gain, qkv_weight)
    shares, message = lax.optimization_barrier((shares, message))
    mine = jnp.sum(shares.astype(F32), axis=0)
    other = lax.ppermute(mine, "core", [(0, 1), (1, 0)])
    message = spread(mine, other, message)
    returned = lax.all_to_all(message, CHIPS, 0, 0, tiled=True)
    dx, grad_qkv, grad_proj, grad_bias, grad_gain = finish(returned, gain, qkv_weight)
    return (
        dx.reshape(activations.shape),
        grad_gain.reshape(256),
        grad_qkv,
        grad_proj,
        grad_bias.reshape(8, 64, 64),
    )


def solution(mesh):
    fine = jax.sharding.Mesh(mesh.devices.reshape(2, 4, 4, 2, 2), (*CHIPS, "core"))
    tokens = P(None, ("zl", "x"), ("y", "zh", "core"), None)
    return jax.shard_map(
        on_device,
        mesh=fine,
        in_specs=(tokens, tokens, P(), P(), P(), P()),
        out_specs=(tokens, P(), P(), P(), P()),
        check_vma=False,
    )
```

time: 131 us -> 113 us (0.86)
  Pallas kernels: 32 us -> 18.7 us
  waiting for transfers between devices: 15.9 us -> 11.2 us
  local copies, waits for them, and re-layouts: 2.58 us -> 0.03 us
  blocking collectives: 71.8 us -> 73.2 us
    pallas_call x2 -> x4, Pallas kernels: 32 us -> 18.7 us  [the longest x1 12.3 us: gradients(): pl.pallas_call(gradients_kernel, out_shape=(jax.ShapeDtypeStruct((64, 16,...]
    all_to_all x1, waiting for transfers between devices: 14.8 us -> 10 us  [on_device(): shares = lax.all_to_all(partials, CHIPS, 0, 0, tiled=True)]
    all_to_all x1, blocking collectives: 30.6 us -> 32.1 us  [on_device(): returned = lax.all_to_all(message, CHIPS, 0, 0, tiled=True)]
  transfers between devices with their start and end apart: 2 -> 2, of which waited for: 2 -> 2; matrix products, arithmetic and copies ran while one was open for 1% -> 0% of each run, Pallas kernels for 0% -> 4%
where the time goes in v2:
time: 113 us
  blocking collectives  73.2 us (65%)
  Pallas kernels  18.7 us (17%)
  waiting for transfers between devices  11.2 us (10%)
  starting transfers between devices  5.76 us (5%)
  other arithmetic  2.98 us (3%)
    all_to_all x1, blocking collectives, on_device(): arrived = lax.all_to_all(both, CHIPS, 0, 0, tiled=True)  41.2 us
    all_to_all x1, blocking collectives, on_device(): returned = lax.all_to_all(message, CHIPS, 0, 0, tiled=True)  32.1 us
    pallas_call x1, Pallas kernels, gradients(): pl.pallas_call(gradients_kernel, out_shape=(jax.ShapeDtypeStruct((64, 16,...  12.3 us
    all_to_all x1, waiting for transfers between devices, on_device(): shares = lax.all_to_all(partials, CHIPS, 0, 0, tiled=True)  10 us
    all_to_all x1, starting transfers between devices, on_device(): shares = lax.all_to_all(partials, CHIPS, 0, 0, tiled=True)  5.68 us
    pallas_call x1, Pallas kernels, input_gradient(): pl.pallas_call(input_kernel, out_shape=jax.ShapeDtypeStruct((64, 16, 512)...  4.48 us
  transfers between devices with their start and end apart: 2, of which 2 were waited for; matrix products, arithmetic and copies ran while one was open for 0% of the time, Pallas kernels for 4%

profile of v2, /device:TPU:0, one launch (start us, length us, event | category | flops | bytes accessed | tf_op | source)
XLA Modules:
  0.0 112.6 jit_solution(6208697969990346932)
XLA Ops:
  0.6 1.7 %pad_maximum_fusion = bf16[64,32,512]{2,1,0:T(8,128)(2,1)S(1)} fusion(bf16[64,32,256]{2,1,0:T(8,128)(2,1)} %bitcast.11, bf16[64,32,256]{2,1,0:T(8,128)(2,1)} %bitcast.12), kind=kLoop, calls=%fused_computation | loop fusion | flops 4194304 | bytes 4194304 | tf_op jit(solution)/shard_map/concatenate | solution.py:306
  2.3 0.0 copy-start
  2.4 0.0 copy-start.1
  2.4 0.0 copy-start.2
  2.4 0.0 copy-start.3
  2.4 41.2 %all_to_all.15.recv = bf16[64,32,512]{2,1,0:T(8,128)(2,1)S(1)} all-to-all(bf16[64,32,512]{2,1,0:T(8,128)(2,1)S(1)} %pad_maximum_fusion), channel_id=1, replica_groups=mesh['zl'=2,'x'=4,'y'=4,'zh'=2,'core'=2] {'zl','x','y','zh'}, dimensions={0} | all-to-all | bytes 4194304 | tf_op jit(solution)/shard_map/all_to_all | solution.py:309
  43.5 0.0 copy-done
  43.5 0.0 copy-done.1
  43.5 0.0 copy-done.2
  43.6 0.0 copy-done.3
  43.6 12.3 %parameter_gradients.1 = (bf16[64,16,384]{2,1,0:T(8,128)(2,1)}, bf16[2048,768]{1,0:T(8,128)(2,1)}) custom-call(bf16[64,32,512]{2,1,0:T(8,128)(2,1)S(1)} %all_to_all.15.recv, f32[1,256]{1,0:T(1,128)S(1)} %bitcast.7, bf16[256,768]{1,0:T(8,128)(2,1)S(1)} %copy-done, bf16[256,256]{1,0:T(8,128)(2,1)S(1)} %copy-done.3, f32[512,64]{1,0:T(8,128)S(1)} %bitcast.10), custom_call_target="tpu_custom_call" | custom-call | flops 8000000000 | bytes 8388608 | tf_op jit(solution)/shard_map/parameter_gradients/pallas_call | solution.py:168
  55.9 5.7 %all-to-all-start.1 = ((bf16[64,16,384]{2,1,0:T(8,128)(2,1)}), bf16[64,16,384]{2,1,0:T(8,128)(2,1)}, u32[]{:S(2)}, u32[]{:S(2)}) async-start(bf16[64,16,384]{2,1,0:T(8,128)(2,1)} %get-tuple-element.14), calls=%async_computation.1 | async-start | bytes 1572864 | tf_op jit(solution)/shard_map/all_to_all | solution.py:314
  61.6 4.5 %input_gradient.1.dx = bf16[64,16,512]{2,1,0:T(8,128)(2,1)S(1)} custom-call(bf16[64,32,512]{2,1,0:T(8,128)(2,1)S(1)} %all_to_all.15.recv, bf16[2048,768]{1,0:T(8,128)(2,1)} %get-tuple-element.15.grad_packed, f32[1,256]{1,0:T(1,128)S(1)} %bitcast.8, bf16[256,768]{1,0:T(8,128)(2,1)S(1)} %copy-done), custom_call_target="tpu_custom_call" | custom-call | flops 6000000000 | bytes 16777216 | tf_op jit(solution)/shard_map/input_gradient/pallas_call | solution.py:224
  66.1 10.0 %all-to-all-done.1 = bf16[64,16,384]{2,1,0:T(8,128)(2,1)} async-done(((bf16[64,16,384]{2,1,0:T(8,128)(2,1)}), bf16[64,16,384]{2,1,0:T(8,128)(2,1)}, u32[]{:S(2)}, u32[]{:S(2)}) %all-to-all-start.1) | async-done | bytes 786464 | tf_op jit(solution)/shard_map/all_to_all | solution.py:314
  76.1 1.3 %convert_reduce_fusion.mine = f32[16,384]{1,0:T(8,128)S(1)} fusion(bf16[64,16,384]{2,1,0:T(8,128)(2,1)} %all-to-all-done.1), kind=kLoop, calls=%fused_computation.1 | loop fusion | flops 780288 | bytes 811008 | tf_op jit(solution)/shard_map/reduce_sum | solution.py:317
  77.4 0.1 collective-permute-start
  77.5 1.2 %collective-permute-done.other = f32[16,384]{1,0:T(8,128)S(1)} collective-permute-done((f32[16,384]{1,0:T(8,128)S(1)}, f32[16,384]{1,0:T(8,128)S(1)}, u32[]{:S(2)}, u32[]{:S(2)}) %collective-permute-start) | collective-permute-done | bytes 24608 | tf_op jit(solution)/shard_map/ppermute | solution.py:318
  78.6 0.2 spread_sums.1
  78.8 32.1 %all_to_all.16.y = bf16[64,16,896]{2,1,0:T(8,128)(2,1)S(1)} all-to-all(bf16[64,16,896]{2,1,0:T(8,128)(2,1)S(1)} %spread_sums.1), channel_id=1, replica_groups=mesh['zl'=2,'x'=4,'y'=4,'zh'=2,'core'=2] {'zl','x','y','zh'}, dimensions={0} | all-to-all | bytes 3670016 | tf_op jit(solution)/shard_map/all_to_all | solution.py:320
  110.9 1.8 %place_results.1 = (bf16[64,32,256]{2,1,0:T(8,128)(2,1)}, f32[256,768]{1,0:T(8,128)}, f32[256,256]{1,0:T(8,128)}, f32[512,64]{1,0:T(8,128)}, f32[1,256]{1,0:T(1,128)}) custom-call(bf16[64,16,896]{2,1,0:T(8,128)(2,1)S(1)} %all_to_all.16.y, f32[1,256]{1,0:T(1,128)S(1)} %bitcast.9, bf16[256,768]{1,0:T(8,128)(2,1)S(1)} %copy-done), custom_call_target="tpu_custom_call" | custom-call | tf_op jit(solution)/shard_map/place_results/pallas_call | solution.py:288
Async XLA Ops:
  2.3 41.2 %copy-start = (bf16[256,768]{1,0:T(8,128)(2,1)S(1)}, bf16[256,768]{1,0:T(8,128)(2,1)}, u32[]{:S(2)}) copy-start(bf16[256,768]{1,0:T(8,128)(2,1)} %wqkv.5) | copy-start | bytes 1179652
  2.4 41.2 %copy-start.1 = (f32[256]{0:T(256)S(1)}, f32[256]{0:T(256)}, u32[]{:S(2)}) copy-start(f32[256]{0:T(256)} %param.8) | copy-start | bytes 3076
  2.4 41.2 %copy-start.2 = (f32[8,64,64]{2,1,0:T(8,128)S(1)}, f32[8,64,64]{2,1,0:T(8,128)}, u32[]{:S(2)}) copy-start(f32[8,64,64]{2,1,0:T(8,128)} %param.11) | copy-start | bytes 393220
  2.4 41.2 %copy-start.3 = (bf16[256,256]{1,0:T(8,128)(2,1)S(1)}, bf16[256,256]{1,0:T(8,128)(2,1)}, u32[]{:S(2)}) copy-start(bf16[256,256]{1,0:T(8,128)(2,1)} %wout.1) | copy-start | bytes 393220
  55.9 20.2 %all-to-all-start.1 = ((bf16[64,16,384]{2,1,0:T(8,128)(2,1)}), bf16[64,16,384]{2,1,0:T(8,128)(2,1)}, u32[]{:S(2)}, u32[]{:S(2)}) async-start(bf16[64,16,384]{2,1,0:T(8,128)(2,1)} %get-tuple-element.14), calls=%async_computation.1 | async-start | bytes 1572864 | tf_op jit(solution)/shard_map/all_to_all | solution.py:314
  77.4 1.3 %collective-permute-start = (f32[16,384]{1,0:T(8,128)S(1)}, f32[16,384]{1,0:T(8,128)S(1)}, u32[]{:S(2)}, u32[]{:S(2)}) collective-permute-start(f32[16,384]{1,0:T(8,128)S(1)} %convert_reduce_fusion.mine), channel_id=1, source_target_pairs={{0,1},{1,0},{2,3},{3,2},{4,5},{5,4},{6,7},{7,6},{8,9},{9,8},{10,11... | collective-permute-start | bytes 73736 | tf_op jit(solution)/shard_map/ppermute | solution.py:318

commit v3 on v2

--- a/solution.py
+++ b/solution.py
@@ -13,6 +13,10 @@
 MEMBERS = 64
 GROUPS = 32
 TOKENS = MEMBERS * GROUPS
+SHARES = 64
+SHARE = 36
+HELD = 40
+ROWS = SHARES * SHARE + HELD - SHARE
 STRIDE = 40
 SCALE = 32**-0.5
 LOG2E = math.log2(math.e)
@@ -31,9 +35,10 @@
 
 def unpack(recv, refs):
     def step(s, _):
-        rows = recv[s]
         for i, ref in enumerate(refs):
-            ref[pl.ds(s * STRIDE, GROUPS), :] = rows[:, 128 * i : 128 * i + 128].astype(F32)
+            first, lane = GROUPS * (i // 2), 128 * (i % 2)
+            rows = recv[s, first : first + GROUPS, lane : lane + 128]
+            ref[pl.ds(s * STRIDE, GROUPS), :] = rows.astype(F32)
         return 0
 
     lax.fori_loop(0, MEMBERS, step, 0, unroll=8)
@@ -110,7 +115,7 @@
 
 def gradients_kernel(
     recv, gain, wqkv, wout, bias, msg, grad_packed,
-    x0, x1, d0, d1, bias_t, grad_bias, normed_s, q_s, k_s, v_s, da_s, dy_s, att_s, gp_s, sem,
+    x0, x1, d0, d1, bias_t, grad_bias, normed_s, q_s, k_s, v_s, da_s, dy_s, att_s, gp_s, rows_s, sem,
 ):
     unpack(recv, (x0, x1, d0, d1))
     for t in range(4):
@@ -148,19 +153,20 @@
             grad_bias[:, 256 * hf : 256 * (hf + 1)] += gb[hf]
         return 0
 
-    lax.fori_loop(0, GROUPS // 8, attend, 0)
+    lax.fori_loop(0, GROUPS // 8, attend, 0, unroll=4)
     copy = pltpu.make_async_copy(gp_s, grad_packed, sem)
     copy.start()
-    grad_qkv = dot(normed_s[...], gp_s[...], TN).astype(BF)
-    grad_proj = dot(att_s[...], dy_s[...], TN).astype(BF)
-    for rb in range(16):
-        rr = slice(16 * rb, 16 * rb + 16)
-        t, j = rb // 4, 16 * (rb % 4)
-        msg[3 * rb] = grad_qkv[rr, 0:384]
-        msg[3 * rb + 1] = grad_qkv[rr, 384:768]
-        msg[3 * rb + 2, :, 0:256] = grad_proj[rr, :]
-        msg[3 * rb + 2, :, 256:384] = grad_bias[j : j + 16, 128 * t : 128 * (t + 1)].astype(BF)
-    msg[48:64] = jnp.zeros((16, 16, 384), BF)
+    grad_qkv = dot(normed_s[...], gp_s[...], TN)
+    grad_proj = dot(att_s[...], dy_s[...], TN)
+    for t in range(6):
+        rows_s[256 * t : 256 * (t + 1), :] = grad_qkv[:, 128 * t : 128 * (t + 1)]
+    for t in range(2):
+        rows_s[256 * (6 + t) : 256 * (7 + t), :] = grad_proj[:, 128 * t : 128 * (t + 1)]
+    for t in range(4):
+        rows_s[2048 + 64 * t : 2112 + 64 * t, :] = grad_bias[:, 128 * t : 128 * (t + 1)]
+    rows_s[SHARES * SHARE :, :] = jnp.zeros((HELD - SHARE, 128), F32)
+    for d in range(SHARES):
+        msg[d] = rows_s[SHARE * d : SHARE * d + HELD, :].astype(BF)
     copy.wait()
 
 
@@ -168,7 +174,7 @@
     return pl.pallas_call(
         gradients_kernel,
         out_shape=(
-            jax.ShapeDtypeStruct((64, 16, 384), BF),
+            jax.ShapeDtypeStruct((SHARES, HELD, 128), BF),
             jax.ShapeDtypeStruct((TOKENS, 768), BF),
         ),
         in_specs=[VM] * 5,
@@ -178,6 +184,7 @@
             *[pltpu.VMEM((MEMBERS, 512), F32)] * 2,
             *[pltpu.VMEM((TOKENS, 256), BF)] * 7,
             pltpu.VMEM((TOKENS, 768), BF),
+            pltpu.VMEM((ROWS, 128), F32),
             pltpu.SemaphoreType.DMA,
         ],
         compiler_params=pltpu.CompilerParams(vmem_limit_bytes=50 * MIB),
@@ -212,9 +219,7 @@
 
     def write(s, _):
         for i, ref in enumerate((x0, x1)):
-            rows = ref[pl.ds(s * STRIDE, GROUPS), :].astype(BF)
-            out[s, :, 128 * i : 128 * i + 128] = rows[:16]
-            out[s, :, 256 + 128 * i : 384 + 128 * i] = rows[16:]
+            out[s, GROUPS * i : GROUPS * (i + 1), :] = ref[pl.ds(s * STRIDE, GROUPS), :].astype(BF)
         return 0
 
     lax.fori_loop(0, MEMBERS, write, 0, unroll=8)
@@ -223,7 +228,7 @@
 def input_gradient(recv, grad_packed, gain, wqkv):
     return pl.pallas_call(
         input_kernel,
-        out_shape=jax.ShapeDtypeStruct((64, 16, 512), BF),
+        out_shape=jax.ShapeDtypeStruct((MEMBERS, 2 * GROUPS, 128), BF),
         in_specs=[VM, HBM, VM, VM],
         out_specs=VM,
         scratch_shapes=[
@@ -243,8 +248,8 @@
     total = (mine[...] + other[...]).astype(BF)
 
     def step(d, _):
-        out[d, :, 0:512] = dx[d]
-        out[d, :, 512:896] = total
+        out[d, 0:64, :] = dx[d]
+        out[d, 64:, :] = total
         return 0
 
     lax.fori_loop(0, 64, step, 0, unroll=8)
@@ -253,7 +258,7 @@
 def spread(mine, other, dx):
     return pl.pallas_call(
         spread_kernel,
-        out_shape=jax.ShapeDtypeStruct((64, 16, 896), BF),
+        out_shape=jax.ShapeDtypeStruct((MEMBERS, 2 * GROUPS + HELD, 128), BF),
         in_specs=[VM] * 3,
         out_specs=VM,
         compiler_params=pltpu.CompilerParams(vmem_limit_bytes=8 * MIB),
@@ -261,24 +266,24 @@
     )(mine, other, dx)
 
 
-def finish_kernel(y, gain, wqkv, dx, qkv, proj, bias, ggain, weight, sem):
+def finish_kernel(y, gain, wqkv, dx, qkv, proj, bias, ggain, rows_s, weight, sem):
     copy = pltpu.make_async_copy(wqkv, weight, sem)
     copy.start()
 
     def step(s, _):
-        dx[s, 0:16, :] = y[s, :, 0:256]
-        dx[s, 16:32, :] = y[s, :, 256:512]
+        dx[s, :, 0:128] = y[s, 0:32, :]
+        dx[s, :, 128:256] = y[s, 32:64, :]
         return 0
 
     lax.fori_loop(0, 64, step, 0, unroll=8)
-    for rb in range(16):
-        rr = slice(16 * rb, 16 * rb + 16)
-        qkv[rr, 0:384] = y[3 * rb, :, 512:896].astype(F32)
-        qkv[rr, 384:768] = y[3 * rb + 1, :, 512:896].astype(F32)
-        proj[rr, :] = y[3 * rb + 2, :, 512:768].astype(F32)
+    for d in range(SHARES):
+        rows_s[SHARE * d : SHARE * d + HELD, :] = y[d, 64:, :].astype(F32)
+    for t in range(6):
+        qkv[:, 128 * t : 128 * (t + 1)] = rows_s[256 * t : 256 * (t + 1), :]
+    for t in range(2):
+        proj[:, 128 * t : 128 * (t + 1)] = rows_s[256 * (6 + t) : 256 * (7 + t), :]
     for t in range(4):
-        tile = [y[(t * 4 + r) * 3 + 2, :, 768:896].astype(F32) for r in range(4)]
-        bias[128 * t : 128 * (t + 1), :] = jnp.concatenate(tile, 0).T
+        bias[128 * t : 128 * (t + 1), :] = rows_s[2048 + 64 * t : 2112 + 64 * t, :].T
     copy.wait()
     along = jnp.sum(qkv[...] * weight[...].astype(F32), -1, keepdims=True)
     ggain[...] = jnp.broadcast_to(along, (256, 128)).T[0:1] / gain[...]
@@ -296,7 +301,11 @@
         ),
         in_specs=[VM, VM, HBM],
         out_specs=(VM,) * 5,
-        scratch_shapes=[pltpu.VMEM((256, 768), BF), pltpu.SemaphoreType.DMA],
+        scratch_shapes=[
+            pltpu.VMEM((ROWS, 128), F32),
+            pltpu.VMEM((256, 768), BF),
+            pltpu.SemaphoreType.DMA,
+        ],
         compiler_params=pltpu.CompilerParams(vmem_limit_bytes=12 * MIB),
         name="place_results",
     )(y, gain, wqkv)
@@ -304,7 +313,7 @@
 
 def on_device(activations, cotangent, ln_gain, qkv_weight, out_weight, position_bias):
     both = jnp.concatenate(
-        [activations.reshape(64, 32, 256), cotangent.reshape(64, 32, 256)], axis=2
+        [activations.reshape(64, 32, 256), cotangent.reshape(64, 32, 256)], axis=1
     )
     arrived = lax.all_to_all(both, CHIPS, 0, 0, tiled=True)
     gain = ln_gain.reshape(1, 256)

time: 113 us -> 110 us (0.973)
  blocking collectives: 73.2 us -> 71.7 us
  waiting for transfers between devices: 11.2 us -> 9.7 us
    all_to_all x1, blocking collectives: 32.1 us -> 30.5 us  [on_device(): returned = lax.all_to_all(message, CHIPS, 0, 0, tiled=True)]
    all_to_all x1, waiting for transfers between devices: 10 us -> 8.53 us  [on_device(): shares = lax.all_to_all(partials, CHIPS, 0, 0, tiled=True)]
where the time goes in v3:
time: 110 us; the launch traced here: 109 us
  blocking collectives  71.7 us (65%)
  Pallas kernels  17.9 us (16%)
  waiting for transfers between devices  9.7 us (9%)
  starting transfers between devices  5.93 us (5%)
  other arithmetic  2.96 us (3%)
    all_to_all x1, blocking collectives, on_device(): arrived = lax.all_to_all(both, CHIPS, 0, 0, tiled=True)  41.2 us
    all_to_all x1, blocking collectives, on_device(): returned = lax.all_to_all(message, CHIPS, 0, 0, tiled=True)  30.5 us
    pallas_call x1, Pallas kernels, gradients(): pl.pallas_call(gradients_kernel, out_shape=(jax.ShapeDtypeStruct((SHARES,...  11.4 us
    all_to_all x1, waiting for transfers between devices, on_device(): shares = lax.all_to_all(partials, CHIPS, 0, 0, tiled=True)  8.53 us
    all_to_all x1, starting transfers between devices, on_device(): shares = lax.all_to_all(partials, CHIPS, 0, 0, tiled=True)  5.85 us
    pallas_call x1, Pallas kernels, input_gradient(): pl.pallas_call(input_kernel, out_shape=jax.ShapeDtypeStruct((MEMBERS, 2 *...  4.44 us
  transfers between devices with their start and end apart: 2, of which 2 were waited for; matrix products, arithmetic and copies ran while one was open for 0% of the time, Pallas kernels for 4%

profile of v3, /device:TPU:0, one launch (start us, length us, event | category | flops | bytes accessed | tf_op | source)
XLA Modules:
  0.0 109.1 jit_solution(16968549248425733287)
XLA Ops:
  0.6 1.8 %pad_maximum_fusion = bf16[64,64,256]{2,1,0:T(8,128)(2,1)S(1)} fusion(bf16[64,32,256]{2,1,0:T(8,128)(2,1)} %bitcast.11, bf16[64,32,256]{2,1,0:T(8,128)(2,1)} %bitcast.12), kind=kLoop, calls=%fused_computation | loop fusion | flops 4194304 | bytes 4194304 | tf_op jit(solution)/shard_map/concatenate | solution.py:315
  2.4 0.0 copy-start
  2.4 0.0 copy-start.1
  2.4 0.0 copy-start.2
  2.4 0.0 copy-start.3
  2.4 41.2 %all_to_all.15.recv = bf16[64,64,256]{2,1,0:T(8,128)(2,1)S(1)} all-to-all(bf16[64,64,256]{2,1,0:T(8,128)(2,1)S(1)} %pad_maximum_fusion), channel_id=1, replica_groups=mesh['zl'=2,'x'=4,'y'=4,'zh'=2,'core'=2] {'zl','x','y','zh'}, dimensions={0} | all-to-all | bytes 4194304 | tf_op jit(solution)/shard_map/all_to_all | solution.py:318
  43.6 0.0 copy-done
  43.6 0.0 copy-done.1
  43.6 0.0 copy-done.2
  43.6 0.0 copy-done.3
  43.6 11.4 %parameter_gradients.1 = (bf16[64,40,128]{2,1,0:T(8,128)(2,1)}, bf16[2048,768]{1,0:T(8,128)(2,1)}) custom-call(bf16[64,64,256]{2,1,0:T(8,128)(2,1)S(1)} %all_to_all.15.recv, f32[1,256]{1,0:T(1,128)S(1)} %bitcast.7, bf16[256,768]{1,0:T(8,128)(2,1)S(1)} %copy-done, bf16[256,256]{1,0:T(8,128)(2,1)S(1)} %copy-done.3, f32[512,64]{1,0:T(8,128)S(1)} %bitcast.10), custom_call_target="tpu_custom_call" | custom-call | flops 8000000000 | bytes 8388608 | tf_op jit(solution)/shard_map/parameter_gradients/pallas_call | solution.py:174
  55.0 5.9 %all-to-all-start.1 = ((bf16[64,40,128]{2,1,0:T(8,128)(2,1)}), bf16[64,40,128]{2,1,0:T(8,128)(2,1)}, u32[]{:S(2)}, u32[]{:S(2)}) async-start(bf16[64,40,128]{2,1,0:T(8,128)(2,1)} %get-tuple-element.14), calls=%async_computation.1 | async-start | bytes 1310720 | tf_op jit(solution)/shard_map/all_to_all | solution.py:323
  60.9 4.4 %input_gradient.1.dx = bf16[64,64,128]{2,1,0:T(8,128)(2,1)S(1)} custom-call(bf16[64,64,256]{2,1,0:T(8,128)(2,1)S(1)} %all_to_all.15.recv, bf16[2048,768]{1,0:T(8,128)(2,1)} %get-tuple-element.15.grad_packed, f32[1,256]{1,0:T(1,128)S(1)} %bitcast.8, bf16[256,768]{1,0:T(8,128)(2,1)S(1)} %copy-done), custom_call_target="tpu_custom_call" | custom-call | flops 6000000000 | bytes 16777216 | tf_op jit(solution)/shard_map/input_gradient/pallas_call | solution.py:229
  65.3 8.5 %all-to-all-done.1 = bf16[64,40,128]{2,1,0:T(8,128)(2,1)} async-done(((bf16[64,40,128]{2,1,0:T(8,128)(2,1)}), bf16[64,40,128]{2,1,0:T(8,128)(2,1)}, u32[]{:S(2)}, u32[]{:S(2)}) %all-to-all-start.1) | async-done | bytes 655392 | tf_op jit(solution)/shard_map/all_to_all | solution.py:323
  73.9 1.2 %convert_reduce_fusion.mine = f32[40,128]{1,0:T(8,128)S(1)} fusion(bf16[64,40,128]{2,1,0:T(8,128)(2,1)} %all-to-all-done.1), kind=kLoop, calls=%fused_computation.1 | loop fusion | flops 650240 | bytes 675840 | tf_op jit(solution)/shard_map/reduce_sum | solution.py:326
  75.1 0.1 collective-permute-start
  75.2 1.2 %collective-permute-done.other = f32[40,128]{1,0:T(8,128)S(1)} collective-permute-done((f32[40,128]{1,0:T(8,128)S(1)}, f32[40,128]{1,0:T(8,128)S(1)}, u32[]{:S(2)}, u32[]{:S(2)}) %collective-permute-start) | collective-permute-done | bytes 20512 | tf_op jit(solution)/shard_map/ppermute | solution.py:327
  76.3 0.1 spread_sums.1
  76.5 30.5 %all_to_all.16.y = bf16[64,104,128]{2,1,0:T(8,128)(2,1)S(1)} all-to-all(bf16[64,104,128]{2,1,0:T(8,128)(2,1)S(1)} %spread_sums.1), channel_id=1, replica_groups=mesh['zl'=2,'x'=4,'y'=4,'zh'=2,'core'=2] {'zl','x','y','zh'}, dimensions={0} | all-to-all | bytes 3407872 | tf_op jit(solution)/shard_map/all_to_all | solution.py:329
  107.0 2.0 %place_results.1 = (bf16[64,32,256]{2,1,0:T(8,128)(2,1)}, f32[256,768]{1,0:T(8,128)}, f32[256,256]{1,0:T(8,128)}, f32[512,64]{1,0:T(8,128)}, f32[1,256]{1,0:T(1,128)}) custom-call(bf16[64,104,128]{2,1,0:T(8,128)(2,1)S(1)} %all_to_all.16.y, f32[1,256]{1,0:T(1,128)S(1)} %bitcast.9, bf16[256,768]{1,0:T(8,128)(2,1)S(1)} %copy-done), custom_call_target="tpu_custom_call" | custom-call | tf_op jit(solution)/shard_map/place_results/pallas_call | solution.py:293
Async XLA Ops:
  2.4 41.2 %copy-start = (bf16[256,768]{1,0:T(8,128)(2,1)S(1)}, bf16[256,768]{1,0:T(8,128)(2,1)}, u32[]{:S(2)}) copy-start(bf16[256,768]{1,0:T(8,128)(2,1)} %wqkv.5) | copy-start | bytes 1179652
  2.4 41.2 %copy-start.1 = (f32[256]{0:T(256)S(1)}, f32[256]{0:T(256)}, u32[]{:S(2)}) copy-start(f32[256]{0:T(256)} %param.8) | copy-start | bytes 3076
  2.4 41.2 %copy-start.2 = (f32[8,64,64]{2,1,0:T(8,128)S(1)}, f32[8,64,64]{2,1,0:T(8,128)}, u32[]{:S(2)}) copy-start(f32[8,64,64]{2,1,0:T(8,128)} %param.11) | copy-start | bytes 393220
  2.4 41.2 %copy-start.3 = (bf16[256,256]{1,0:T(8,128)(2,1)S(1)}, bf16[256,256]{1,0:T(8,128)(2,1)}, u32[]{:S(2)}) copy-start(bf16[256,256]{1,0:T(8,128)(2,1)} %wout.1) | copy-start | bytes 393220
  55.0 18.8 %all-to-all-start.1 = ((bf16[64,40,128]{2,1,0:T(8,128)(2,1)}), bf16[64,40,128]{2,1,0:T(8,128)(2,1)}, u32[]{:S(2)}, u32[]{:S(2)}) async-start(bf16[64,40,128]{2,1,0:T(8,128)(2,1)} %get-tuple-element.14), calls=%async_computation.1 | async-start | bytes 1310720 | tf_op jit(solution)/shard_map/all_to_all | solution.py:323
  75.1 1.3 %collective-permute-start = (f32[40,128]{1,0:T(8,128)S(1)}, f32[40,128]{1,0:T(8,128)S(1)}, u32[]{:S(2)}, u32[]{:S(2)}) collective-permute-start(f32[40,128]{1,0:T(8,128)S(1)} %convert_reduce_fusion.mine), channel_id=1, source_target_pairs={{0,1},{1,0},{2,3},{3,2},{4,5},{5,4},{6,7},{7,6},{8,9},{9,8},{10,11... | collective-permute-start | bytes 61448 | tf_op jit(solution)/shard_map/ppermute | solution.py:327

commit v4 on v3

--- a/solution.py
+++ b/solution.py
@@ -84,31 +84,35 @@
         g, hf = u
         return a[MEMBERS * g : MEMBERS * (g + 1), 128 * hf : 128 * (hf + 1)]
 
-    qx = {u: expand(part(q, u), masks) for u in units}
-    dax = {u: expand(part(da, u), masks) for u in units}
-    scores = {}
-    grad_probs = {}
+    def diagonal(a, b):
+        zero = jnp.zeros_like(a)
+        top = jnp.concatenate([a, zero], axis=1)
+        return jnp.concatenate([top, jnp.concatenate([zero, b], axis=1)], axis=0)
+
+    wide = {}
+    products = {}
     for u in units:
-        scores[u] = dot(part(k, u), qx[u], NT)
-        grad_probs[u] = dot(part(v, u), dax[u], NT)
-    weights = {}
-    scaled = {}
+        wide[u] = jnp.concatenate([expand(part(q, u), masks), expand(part(da, u), masks)], axis=1)
+        products[u] = dot(diagonal(part(k, u), part(v, u)), wide[u], NT)
+    stacked = {}
     grad_bias = [None, None]
     for u in units:
         hf = u[1]
-        logits = scores[u] + bias[:, 256 * hf : 256 * (hf + 1)]
+        logits = products[u][:MEMBERS] + bias[:, 256 * hf : 256 * (hf + 1)]
+        grad_probs = products[u][MEMBERS:]
         e = jnp.exp2(logits - jnp.max(logits, 0, keepdims=True))
         p = e * (1.0 / jnp.sum(e, 0, keepdims=True))
-        ds = p * (grad_probs[u] - jnp.sum(grad_probs[u] * p, 0, keepdims=True))
-        weights[u] = p.astype(BF)
-        scaled[u] = ds.astype(BF)
+        ds = p * (grad_probs - jnp.sum(grad_probs * p, 0, keepdims=True))
+        stacked[u] = jnp.concatenate([p.astype(BF), ds.astype(BF)], axis=0)
         grad_bias[hf] = ds if grad_bias[hf] is None else grad_bias[hf] + ds
     results = {}
     for u in units:
-        attended = pick(dot(weights[u], part(v, u), TN), masks)
-        grad_v = dot(weights[u], dax[u], NN)
-        grad_k = dot(scaled[u], qx[u], NN) * (1.0 / LOG2E)
-        grad_q = pick(dot(scaled[u], part(k, u), TN), masks) * SCALE
+        down = dot(stacked[u], wide[u], NN)
+        grad_v = down[:MEMBERS, 128:]
+        grad_k = down[MEMBERS:, :128] * (1.0 / LOG2E)
+        across = dot(stacked[u], diagonal(part(v, u), part(k, u)), TN)
+        attended = pick(across[:, :128], masks)
+        grad_q = pick(across[:, 128:], masks) * SCALE
         results[u] = [r.astype(BF) for r in (attended, grad_q, grad_k, grad_v)]
     return results, grad_bias
 
@@ -139,6 +143,10 @@
 
     lax.fori_loop(0, GROUPS // 8, project, 0, unroll=4)
 
+    def keep(b):
+        rows = pl.ds(pl.multiple_of(b * 512, 512), 512)
+        return pltpu.make_async_copy(gp_s.at[rows, :], grad_packed.at[rows, :], sem.at[b])
+
     def attend(b, _):
         rows = pl.ds(pl.multiple_of(b * 512, 512), 512)
         results, gb = attention(
@@ -151,11 +159,10 @@
                 gp_s[r, 256 * i + 128 * hf : 256 * i + 128 * (hf + 1)] = part
         for hf in range(2):
             grad_bias[:, 256 * hf : 256 * (hf + 1)] += gb[hf]
+        keep(b).start()
         return 0
 
     lax.fori_loop(0, GROUPS // 8, attend, 0, unroll=4)
-    copy = pltpu.make_async_copy(gp_s, grad_packed, sem)
-    copy.start()
     grad_qkv = dot(normed_s[...], gp_s[...], TN)
     grad_proj = dot(att_s[...], dy_s[...], TN)
     for t in range(6):
@@ -167,7 +174,8 @@
     rows_s[SHARES * SHARE :, :] = jnp.zeros((HELD - SHARE, 128), F32)
     for d in range(SHARES):
         msg[d] = rows_s[SHARE * d : SHARE * d + HELD, :].astype(BF)
-    copy.wait()
+    for b in range(GROUPS // 8):
+        keep(b).wait()
 
 
 def gradients(recv, gain, wqkv, wout, bias):
@@ -185,7 +193,7 @@
             *[pltpu.VMEM((TOKENS, 256), BF)] * 7,
             pltpu.VMEM((TOKENS, 768), BF),
             pltpu.VMEM((ROWS, 128), F32),
-            pltpu.SemaphoreType.DMA,
+            pltpu.SemaphoreType.DMA((GROUPS // 8,)),
         ],
         compiler_params=pltpu.CompilerParams(vmem_limit_bytes=50 * MIB),
         cost_estimate=pl.CostEstimate(

time: 110 us -> 108 us (0.982)
  Pallas kernels: 17.9 us -> 16.4 us
    pallas_call x1, Pallas kernels: 11.4 us -> 9.82 us  [gradients(): pl.pallas_call(gradients_kernel, out_shape=(jax.ShapeDtypeStruct((SHARES,...]
where the time goes in v4:
time: 108 us
  blocking collectives  71.7 us (66%)
  Pallas kernels  16.4 us (15%)
  waiting for transfers between devices  9.69 us (9%)
  starting transfers between devices  5.94 us (6%)
  other arithmetic  2.96 us (3%)
    all_to_all x1, blocking collectives, on_device(): arrived = lax.all_to_all(both, CHIPS, 0, 0, tiled=True)  41.2 us
    all_to_all x1, blocking collectives, on_device(): returned = lax.all_to_all(message, CHIPS, 0, 0, tiled=True)  30.5 us
    pallas_call x1, Pallas kernels, gradients(): pl.pallas_call(gradients_kernel, out_shape=(jax.ShapeDtypeStruct((SHARES,...  9.82 us
    all_to_all x1, waiting for transfers between devices, on_device(): shares = lax.all_to_all(partials, CHIPS, 0, 0, tiled=True)  8.52 us
    all_to_all x1, starting transfers between devices, on_device(): shares = lax.all_to_all(partials, CHIPS, 0, 0, tiled=True)  5.86 us
    pallas_call x1, Pallas kernels, input_gradient(): pl.pallas_call(input_kernel, out_shape=jax.ShapeDtypeStruct((MEMBERS, 2 *...  4.44 us
  transfers between devices with their start and end apart: 2, of which 2 were waited for; matrix products, arithmetic and copies ran while one was open for 0% of the time, Pallas kernels for 4%

profile of v4, /device:TPU:0, one launch (start us, length us, event | category | flops | bytes accessed | tf_op | source)
XLA Modules:
  0.0 107.6 jit_solution(4675002754650866303)
XLA Ops:
  0.6 1.8 %pad_maximum_fusion = bf16[64,64,256]{2,1,0:T(8,128)(2,1)S(1)} fusion(bf16[64,32,256]{2,1,0:T(8,128)(2,1)} %bitcast.11, bf16[64,32,256]{2,1,0:T(8,128)(2,1)} %bitcast.12), kind=kLoop, calls=%fused_computation | loop fusion | flops 4194304 | bytes 4194304 | tf_op jit(solution)/shard_map/concatenate | solution.py:323
  2.4 0.0 copy-start
  2.4 0.0 copy-start.1
  2.4 0.0 copy-start.2
  2.4 0.0 copy-start.3
  2.4 41.2 %all_to_all.15.recv = bf16[64,64,256]{2,1,0:T(8,128)(2,1)S(1)} all-to-all(bf16[64,64,256]{2,1,0:T(8,128)(2,1)S(1)} %pad_maximum_fusion), channel_id=1, replica_groups=mesh['zl'=2,'x'=4,'y'=4,'zh'=2,'core'=2] {'zl','x','y','zh'}, dimensions={0} | all-to-all | bytes 4194304 | tf_op jit(solution)/shard_map/all_to_all | solution.py:326
  43.6 0.0 copy-done
  43.6 0.0 copy-done.1
  43.6 0.0 copy-done.2
  43.6 0.0 copy-done.3
  43.6 9.8 %parameter_gradients.1 = (bf16[64,40,128]{2,1,0:T(8,128)(2,1)}, bf16[2048,768]{1,0:T(8,128)(2,1)}) custom-call(bf16[64,64,256]{2,1,0:T(8,128)(2,1)S(1)} %all_to_all.15.recv, f32[1,256]{1,0:T(1,128)S(1)} %bitcast.7, bf16[256,768]{1,0:T(8,128)(2,1)S(1)} %copy-done, bf16[256,256]{1,0:T(8,128)(2,1)S(1)} %copy-done.3, f32[512,64]{1,0:T(8,128)S(1)} %bitcast.10), custom_call_target="tpu_custom_call" | custom-call | flops 8000000000 | bytes 8388608 | tf_op jit(solution)/shard_map/parameter_gradients/pallas_call | solution.py:182
  53.4 5.9 %all-to-all-start.1 = ((bf16[64,40,128]{2,1,0:T(8,128)(2,1)}), bf16[64,40,128]{2,1,0:T(8,128)(2,1)}, u32[]{:S(2)}, u32[]{:S(2)}) async-start(bf16[64,40,128]{2,1,0:T(8,128)(2,1)} %get-tuple-element.14), calls=%async_computation.1 | async-start | bytes 1310720 | tf_op jit(solution)/shard_map/all_to_all | solution.py:331
  59.3 4.4 %input_gradient.1.dx = bf16[64,64,128]{2,1,0:T(8,128)(2,1)S(1)} custom-call(bf16[64,64,256]{2,1,0:T(8,128)(2,1)S(1)} %all_to_all.15.recv, bf16[2048,768]{1,0:T(8,128)(2,1)} %get-tuple-element.15.grad_packed, f32[1,256]{1,0:T(1,128)S(1)} %bitcast.8, bf16[256,768]{1,0:T(8,128)(2,1)S(1)} %copy-done), custom_call_target="tpu_custom_call" | custom-call | flops 6000000000 | bytes 16777216 | tf_op jit(solution)/shard_map/input_gradient/pallas_call | solution.py:237
  63.8 8.5 %all-to-all-done.1 = bf16[64,40,128]{2,1,0:T(8,128)(2,1)} async-done(((bf16[64,40,128]{2,1,0:T(8,128)(2,1)}), bf16[64,40,128]{2,1,0:T(8,128)(2,1)}, u32[]{:S(2)}, u32[]{:S(2)}) %all-to-all-start.1) | async-done | bytes 655392 | tf_op jit(solution)/shard_map/all_to_all | solution.py:331
  72.3 1.2 %convert_reduce_fusion.mine = f32[40,128]{1,0:T(8,128)S(1)} fusion(bf16[64,40,128]{2,1,0:T(8,128)(2,1)} %all-to-all-done.1), kind=kLoop, calls=%fused_computation.1 | loop fusion | flops 650240 | bytes 675840 | tf_op jit(solution)/shard_map/reduce_sum | solution.py:334
  73.5 0.1 collective-permute-start
  73.6 1.2 %collective-permute-done.other = f32[40,128]{1,0:T(8,128)S(1)} collective-permute-done((f32[40,128]{1,0:T(8,128)S(1)}, f32[40,128]{1,0:T(8,128)S(1)}, u32[]{:S(2)}, u32[]{:S(2)}) %collective-permute-start) | collective-permute-done | bytes 20512 | tf_op jit(solution)/shard_map/ppermute | solution.py:335
  74.8 0.1 spread_sums.1
  74.9 30.5 %all_to_all.16.y = bf16[64,104,128]{2,1,0:T(8,128)(2,1)S(1)} all-to-all(bf16[64,104,128]{2,1,0:T(8,128)(2,1)S(1)} %spread_sums.1), channel_id=1, replica_groups=mesh['zl'=2,'x'=4,'y'=4,'zh'=2,'core'=2] {'zl','x','y','zh'}, dimensions={0} | all-to-all | bytes 3407872 | tf_op jit(solution)/shard_map/all_to_all | solution.py:337
  105.4 2.0 %place_results.1 = (bf16[64,32,256]{2,1,0:T(8,128)(2,1)}, f32[256,768]{1,0:T(8,128)}, f32[256,256]{1,0:T(8,128)}, f32[512,64]{1,0:T(8,128)}, f32[1,256]{1,0:T(1,128)}) custom-call(bf16[64,104,128]{2,1,0:T(8,128)(2,1)S(1)} %all_to_all.16.y, f32[1,256]{1,0:T(1,128)S(1)} %bitcast.9, bf16[256,768]{1,0:T(8,128)(2,1)S(1)} %copy-done), custom_call_target="tpu_custom_call" | custom-call | tf_op jit(solution)/shard_map/place_results/pallas_call | solution.py:301
Async XLA Ops:
  2.4 41.2 %copy-start = (bf16[256,768]{1,0:T(8,128)(2,1)S(1)}, bf16[256,768]{1,0:T(8,128)(2,1)}, u32[]{:S(2)}) copy-start(bf16[256,768]{1,0:T(8,128)(2,1)} %wqkv.5) | copy-start | bytes 1179652
  2.4 41.2 %copy-start.1 = (f32[256]{0:T(256)S(1)}, f32[256]{0:T(256)}, u32[]{:S(2)}) copy-start(f32[256]{0:T(256)} %param.8) | copy-start | bytes 3076
  2.4 41.2 %copy-start.2 = (f32[8,64,64]{2,1,0:T(8,128)S(1)}, f32[8,64,64]{2,1,0:T(8,128)}, u32[]{:S(2)}) copy-start(f32[8,64,64]{2,1,0:T(8,128)} %param.11) | copy-start | bytes 393220
  2.4 41.2 %copy-start.3 = (bf16[256,256]{1,0:T(8,128)(2,1)S(1)}, bf16[256,256]{1,0:T(8,128)(2,1)}, u32[]{:S(2)}) copy-start(bf16[256,256]{1,0:T(8,128)(2,1)} %wout.1) | copy-start | bytes 393220
  53.4 18.8 %all-to-all-start.1 = ((bf16[64,40,128]{2,1,0:T(8,128)(2,1)}), bf16[64,40,128]{2,1,0:T(8,128)(2,1)}, u32[]{:S(2)}, u32[]{:S(2)}) async-start(bf16[64,40,128]{2,1,0:T(8,128)(2,1)} %get-tuple-element.14), calls=%async_computation.1 | async-start | bytes 1310720 | tf_op jit(solution)/shard_map/all_to_all | solution.py:331
  73.5 1.3 %collective-permute-start = (f32[40,128]{1,0:T(8,128)S(1)}, f32[40,128]{1,0:T(8,128)S(1)}, u32[]{:S(2)}, u32[]{:S(2)}) collective-permute-start(f32[40,128]{1,0:T(8,128)S(1)} %convert_reduce_fusion.mine), channel_id=1, source_target_pairs={{0,1},{1,0},{2,3},{3,2},{4,5},{5,4},{6,7},{7,6},{8,9},{9,8},{10,11... | collective-permute-start | bytes 61448 | tf_op jit(solution)/shard_map/ppermute | solution.py:335

commit v5 on v4

--- a/solution.py
+++ b/solution.py
@@ -118,8 +118,8 @@
 
 
 def gradients_kernel(
-    recv, gain, wqkv, wout, bias, msg, grad_packed,
-    x0, x1, d0, d1, bias_t, grad_bias, normed_s, q_s, k_s, v_s, da_s, dy_s, att_s, gp_s, rows_s, sem,
+    recv, gain, wqkv, wout, bias, msg, x0, x1, d0, d1, bias_t, grad_bias,
+    normal_s, inverse_s, normed_s, q_s, k_s, v_s, da_s, dy_s, att_s, gp_s, rows_s,
 ):
     unpack(recv, (x0, x1, d0, d1))
     for t in range(4):
@@ -132,7 +132,9 @@
         dy = grouped((d0, d1), b * 8, 8).astype(BF)
         dy_s[rows, :] = dy
         da_s[rows, :] = dot(dy, wout[...], NT).astype(BF)
-        normal, _ = normalise(grouped((x0, x1), b * 8, 8))
+        normal, inverse = normalise(grouped((x0, x1), b * 8, 8))
+        normal_s[rows, :] = normal
+        inverse_s[rows, :] = jnp.broadcast_to(inverse, (512, 128))
         normed = (normal * gain[...]).astype(BF)
         normed_s[rows, :] = normed
         packed = dot(normed, wqkv[...], NN)
@@ -142,10 +144,6 @@
         return 0
 
     lax.fori_loop(0, GROUPS // 8, project, 0, unroll=4)
-
-    def keep(b):
-        rows = pl.ds(pl.multiple_of(b * 512, 512), 512)
-        return pltpu.make_async_copy(gp_s.at[rows, :], grad_packed.at[rows, :], sem.at[b])
 
     def attend(b, _):
         rows = pl.ds(pl.multiple_of(b * 512, 512), 512)
@@ -159,7 +157,6 @@
                 gp_s[r, 256 * i + 128 * hf : 256 * i + 128 * (hf + 1)] = part
         for hf in range(2):
             grad_bias[:, 256 * hf : 256 * (hf + 1)] += gb[hf]
-        keep(b).start()
         return 0
 
     lax.fori_loop(0, GROUPS // 8, attend, 0, unroll=4)
@@ -173,49 +170,16 @@
         rows_s[2048 + 64 * t : 2112 + 64 * t, :] = grad_bias[:, 128 * t : 128 * (t + 1)]
     rows_s[SHARES * SHARE :, :] = jnp.zeros((HELD - SHARE, 128), F32)
     for d in range(SHARES):
-        msg[d] = rows_s[SHARE * d : SHARE * d + HELD, :].astype(BF)
-    for b in range(GROUPS // 8):
-        keep(b).wait()
-
-
-def gradients(recv, gain, wqkv, wout, bias):
-    return pl.pallas_call(
-        gradients_kernel,
-        out_shape=(
-            jax.ShapeDtypeStruct((SHARES, HELD, 128), BF),
-            jax.ShapeDtypeStruct((TOKENS, 768), BF),
-        ),
-        in_specs=[VM] * 5,
-        out_specs=(VM, HBM),
-        scratch_shapes=[
-            *[pltpu.VMEM((MEMBERS * STRIDE, 128), F32)] * 4,
-            *[pltpu.VMEM((MEMBERS, 512), F32)] * 2,
-            *[pltpu.VMEM((TOKENS, 256), BF)] * 7,
-            pltpu.VMEM((TOKENS, 768), BF),
-            pltpu.VMEM((ROWS, 128), F32),
-            pltpu.SemaphoreType.DMA((GROUPS // 8,)),
-        ],
-        compiler_params=pltpu.CompilerParams(vmem_limit_bytes=50 * MIB),
-        cost_estimate=pl.CostEstimate(
-            flops=8 * 10**9, bytes_accessed=8 * 2**20, transcendentals=8 * 2**20
-        ),
-        name="parameter_gradients",
-    )(recv, gain, wqkv, wout, bias)
-
-
-def input_kernel(recv, grad_packed, gain, wqkv, out, x0, x1, d0, d1, gp_s, sem):
-    copy = pltpu.make_async_copy(grad_packed, gp_s, sem)
-    copy.start()
-    unpack(recv, (x0, x1, d0, d1))
-    copy.wait()
-
-    def block(b, _):
+        msg[d, 2 * GROUPS :, :] = rows_s[SHARE * d : SHARE * d + HELD, :].astype(BF)
+
+    def pull_back(b, _):
         rows = pl.ds(pl.multiple_of(b * 512, 512), 512)
         g = dot(gp_s[rows, :], wqkv[...], NT) * gain[...]
-        normal, inverse = normalise(grouped((x0, x1), b * 8, 8))
+        normal = normal_s[rows, :]
+        inverse = jnp.concatenate([inverse_s[rows, :]] * 2, axis=1)
         along = jnp.mean(g * normal, -1, keepdims=True)
         dx = inverse * (g - jnp.mean(g, -1, keepdims=True) - normal * along)
-        dx = grouped((d0, d1), b * 8, 8) + dx
+        dx = dy_s[rows, :].astype(F32) + dx
         for k in range(8):
             for i, ref in enumerate((x0, x1)):
                 ref[pl.ds(b * 8 + k, MEMBERS, stride=STRIDE), :] = dx[
@@ -223,58 +187,37 @@
                 ]
         return 0
 
-    lax.fori_loop(0, GROUPS // 8, block, 0, unroll=4)
+    lax.fori_loop(0, GROUPS // 8, pull_back, 0, unroll=4)
 
     def write(s, _):
         for i, ref in enumerate((x0, x1)):
-            out[s, GROUPS * i : GROUPS * (i + 1), :] = ref[pl.ds(s * STRIDE, GROUPS), :].astype(BF)
+            msg[s, GROUPS * i : GROUPS * (i + 1), :] = ref[pl.ds(s * STRIDE, GROUPS), :].astype(BF)
         return 0
 
     lax.fori_loop(0, MEMBERS, write, 0, unroll=8)
 
 
-def input_gradient(recv, grad_packed, gain, wqkv):
+def gradients(recv, gain, wqkv, wout, bias):
     return pl.pallas_call(
-        input_kernel,
-        out_shape=jax.ShapeDtypeStruct((MEMBERS, 2 * GROUPS, 128), BF),
-        in_specs=[VM, HBM, VM, VM],
+        gradients_kernel,
+        out_shape=jax.ShapeDtypeStruct((MEMBERS, 2 * GROUPS + HELD, 128), BF),
+        in_specs=[VM] * 5,
         out_specs=VM,
         scratch_shapes=[
             *[pltpu.VMEM((MEMBERS * STRIDE, 128), F32)] * 4,
+            *[pltpu.VMEM((MEMBERS, 512), F32)] * 2,
+            pltpu.VMEM((TOKENS, 256), F32),
+            pltpu.VMEM((TOKENS, 128), F32),
+            *[pltpu.VMEM((TOKENS, 256), BF)] * 7,
             pltpu.VMEM((TOKENS, 768), BF),
-            pltpu.SemaphoreType.DMA,
+            pltpu.VMEM((ROWS, 128), F32),
         ],
-        compiler_params=pltpu.CompilerParams(vmem_limit_bytes=50 * MIB),
-        cost_estimate=pl.CostEstimate(
-            flops=6 * 10**9, bytes_accessed=16 * 2**20, transcendentals=2**20
-        ),
-        name="input_gradient",
-    )(recv, grad_packed, gain, wqkv)
-
-
-def spread_kernel(mine, other, dx, out):
-    total = (mine[...] + other[...]).astype(BF)
-
-    def step(d, _):
-        out[d, 0:64, :] = dx[d]
-        out[d, 64:, :] = total
-        return 0
-
-    lax.fori_loop(0, 64, step, 0, unroll=8)
-
-
-def spread(mine, other, dx):
-    return pl.pallas_call(
-        spread_kernel,
-        out_shape=jax.ShapeDtypeStruct((MEMBERS, 2 * GROUPS + HELD, 128), BF),
-        in_specs=[VM] * 3,
-        out_specs=VM,
-        compiler_params=pltpu.CompilerParams(vmem_limit_bytes=8 * MIB),
-        name="spread_sums",
-    )(mine, other, dx)
-
-
-def finish_kernel(y, gain, wqkv, dx, qkv, proj, bias, ggain, rows_s, weight, sem):
+        compiler_params=pltpu.CompilerParams(vmem_limit_bytes=40 * MIB),
+        name="layer_gradients",
+    )(recv, gain, wqkv, wout, bias)
+
+
+def finish_kernel(y, sums, gain, wqkv, dx, qkv, proj, bias, ggain, rows_s, weight, sem):
     copy = pltpu.make_async_copy(wqkv, weight, sem)
     copy.start()
 
@@ -285,19 +228,27 @@
 
     lax.fori_loop(0, 64, step, 0, unroll=8)
     for d in range(SHARES):
-        rows_s[SHARE * d : SHARE * d + HELD, :] = y[d, 64:, :].astype(F32)
-    for t in range(6):
-        qkv[:, 128 * t : 128 * (t + 1)] = rows_s[256 * t : 256 * (t + 1), :]
-    for t in range(2):
-        proj[:, 128 * t : 128 * (t + 1)] = rows_s[256 * (6 + t) : 256 * (7 + t), :]
+        share = sums[d].astype(F32)
+        row = SHARE * d
+        while row < SHARE * (d + 1):
+            t, r = divmod(row, 256)
+            count = min(256 - r, SHARE * (d + 1) - row)
+            part = share[row - SHARE * d : row - SHARE * d + count]
+            if t < 6:
+                qkv[r : r + count, 128 * t : 128 * (t + 1)] = part
+            elif t < 8:
+                proj[r : r + count, 128 * (t - 6) : 128 * (t - 5)] = part
+            else:
+                rows_s[r : r + count, :] = part
+            row += count
     for t in range(4):
-        bias[128 * t : 128 * (t + 1), :] = rows_s[2048 + 64 * t : 2112 + 64 * t, :].T
+        bias[128 * t : 128 * (t + 1), :] = rows_s[64 * t : 64 * (t + 1), :].T
     copy.wait()
     along = jnp.sum(qkv[...] * weight[...].astype(F32), -1, keepdims=True)
     ggain[...] = jnp.broadcast_to(along, (256, 128)).T[0:1] / gain[...]
 
 
-def finish(y, gain, wqkv):
+def finish(y, sums, gain, wqkv):
     return pl.pallas_call(
         finish_kernel,
         out_shape=(
@@ -307,16 +258,16 @@
             jax.ShapeDtypeStruct((512, 64), F32),
             jax.ShapeDtypeStruct((1, 256), F32),
         ),
-        in_specs=[VM, VM, HBM],
+        in_specs=[VM, VM, VM, HBM],
         out_specs=(VM,) * 5,
         scratch_shapes=[
-            pltpu.VMEM((ROWS, 128), F32),
+            pltpu.VMEM((256, 128), F32),
             pltpu.VMEM((256, 768), BF),
             pltpu.SemaphoreType.DMA,
         ],
         compiler_params=pltpu.CompilerParams(vmem_limit_bytes=12 * MIB),
         name="place_results",
-    )(y, gain, wqkv)
+    )(y, sums, gain, wqkv)
 
 
 def on_device(activations, cotangent, ln_gain, qkv_weight, out_weight, position_bias):
@@ -325,17 +276,13 @@
     )
     arrived = lax.all_to_all(both, CHIPS, 0, 0, tiled=True)
     gain = ln_gain.reshape(1, 256)
-    partials, grad_packed = gradients(
-        arrived, gain, qkv_weight, out_weight, position_bias.reshape(512, 64)
-    )
-    shares = lax.all_to_all(partials, CHIPS, 0, 0, tiled=True)
-    message = input_gradient(arrived, grad_packed, gain, qkv_weight)
-    shares, message = lax.optimization_barrier((shares, message))
-    mine = jnp.sum(shares.astype(F32), axis=0)
+    message = gradients(arrived, gain, qkv_weight, out_weight, position_bias.reshape(512, 64))
+    returned = lax.all_to_all(message, CHIPS, 0, 0, tiled=True)
+    mine = jnp.sum(returned[:, 2 * GROUPS :, :].astype(F32), axis=0)
     other = lax.ppermute(mine, "core", [(0, 1), (1, 0)])
-    message = spread(mine, other, message)
-    returned = lax.all_to_all(message, CHIPS, 0, 0, tiled=True)
-    dx, grad_qkv, grad_proj, grad_bias, grad_gain = finish(returned, gain, qkv_weight)
+    total = jnp.broadcast_to((mine + other).astype(BF), (SHARES, HELD, 128))
+    sums = lax.all_to_all(total, CHIPS, 0, 0, tiled=True)
+    dx, grad_qkv, grad_proj, grad_bias, grad_gain = finish(returned, sums, gain, qkv_weight)
     return (
         dx.reshape(activations.shape),
         grad_gain.reshape(256),

time: 108 us -> 107 us (level)
  blocking collectives: 71.7 us -> 90.2 us
  waiting for transfers between devices: 9.69 us -> 1.18 us
  starting transfers between devices: 5.94 us -> 0.08 us
  Pallas kernels: 16.4 us -> 12.6 us
  other arithmetic: 2.96 us -> 1.88 us
    all_to_all x0 -> x1, blocking collectives: none -> 19.8 us  [on_device(): sums = lax.all_to_all(total, CHIPS, 0, 0, tiled=True)]
    all_to_all x1 -> x0, waiting for transfers between devices: 8.52 us -> none  [on_device(): shares = lax.all_to_all(partials, CHIPS, 0, 0, tiled=True)]
    all_to_all x1 -> x0, starting transfers between devices: 5.86 us -> none  [on_device(): shares = lax.all_to_all(partials, CHIPS, 0, 0, tiled=True)]
    pallas_call x3 -> x1, Pallas kernels: 14.4 us -> 10.6 us  [gradients(): pl.pallas_call(gradients_kernel, out_shape=jax.ShapeDtypeStruct((MEMBERS,...]
    all_to_all x1, blocking collectives: 30.5 us -> 29.3 us  [on_device(): returned = lax.all_to_all(message, CHIPS, 0, 0, tiled=True)]
    reduce_sum x1, other arithmetic: 1.21 us -> 0.12 us  [on_device(): mine = jnp.sum(returned[:, 2 * GROUPS:, :].astype(F32), axis=0)]
  transfers between devices with their start and end apart: 2 -> 1, of which waited for: 2 -> 1; matrix products, arithmetic and copies ran while one was open for 0% -> 0% of each run, Pallas kernels for 4% -> 0%
where the time goes in v5:
time: 107 us
  blocking collectives  90.2 us (84%)
  Pallas kernels  12.6 us (12%)
  other arithmetic  1.88 us (2%)
  waiting for transfers between devices  1.18 us (1%)
    all_to_all x1, blocking collectives, on_device(): arrived = lax.all_to_all(both, CHIPS, 0, 0, tiled=True)  41.2 us
    all_to_all x1, blocking collectives, on_device(): returned = lax.all_to_all(message, CHIPS, 0, 0, tiled=True)  29.3 us
    all_to_all x1, blocking collectives, on_device(): sums = lax.all_to_all(total, CHIPS, 0, 0, tiled=True)  19.8 us
    pallas_call x1, Pallas kernels, gradients(): pl.pallas_call(gradients_kernel, out_shape=jax.ShapeDtypeStruct((MEMBERS,...  10.6 us
  transfers between devices with their start and end apart: 1, of which 1 were waited for; matrix products, arithmetic and copies ran while one was open for 0% of the time, Pallas kernels for 0%

profile of v5, /device:TPU:0, one launch (start us, length us, event | category | flops | bytes accessed | tf_op | source)
XLA Modules:
  0.0 106.8 jit_solution(12836644594216394345)
XLA Ops:
  0.6 1.8 %pad_maximum_fusion = bf16[64,64,256]{2,1,0:T(8,128)(2,1)S(1)} fusion(bf16[64,32,256]{2,1,0:T(8,128)(2,1)} %bitcast.10, bf16[64,32,256]{2,1,0:T(8,128)(2,1)} %bitcast.11), kind=kLoop, calls=%fused_computation | loop fusion | flops 4194304 | bytes 4194304 | tf_op jit(solution)/shard_map/concatenate | solution.py:274
  2.4 0.0 copy-start
  2.4 0.0 copy-start.1
  2.4 0.0 copy-start.2
  2.4 0.0 copy-start.3
  2.4 41.2 %all_to_all.15.recv = bf16[64,64,256]{2,1,0:T(8,128)(2,1)S(1)} all-to-all(bf16[64,64,256]{2,1,0:T(8,128)(2,1)S(1)} %pad_maximum_fusion), channel_id=1, replica_groups=mesh['zl'=2,'x'=4,'y'=4,'zh'=2,'core'=2] {'zl','x','y','zh'}, dimensions={0} | all-to-all | bytes 4194304 | tf_op jit(solution)/shard_map/all_to_all | solution.py:277
  43.6 0.0 copy-done
  43.6 0.0 copy-done.1
  43.6 0.0 copy-done.2
  43.6 0.0 copy-done.3
  43.6 10.6 %layer_gradients.1 = bf16[64,104,128]{2,1,0:T(8,128)(2,1)S(1)} custom-call(bf16[64,64,256]{2,1,0:T(8,128)(2,1)S(1)} %all_to_all.15.recv, f32[1,256]{1,0:T(1,128)S(1)} %bitcast.8, bf16[256,768]{1,0:T(8,128)(2,1)S(1)} %copy-done, bf16[256,256]{1,0:T(8,128)(2,1)S(1)} %copy-done.2, f32[512,64]{1,0:T(8,128)S(1)} %bitcast.7), custom_call_target="tpu_custom_call" | custom-call | tf_op jit(solution)/shard_map/layer_gradients/pallas_call | solution.py:201
  54.3 29.3 %all_to_all.16.y = bf16[64,104,128]{2,1,0:T(8,128)(2,1)S(1)} all-to-all(bf16[64,104,128]{2,1,0:T(8,128)(2,1)S(1)} %layer_gradients.1), channel_id=1, replica_groups=mesh['zl'=2,'x'=4,'y'=4,'zh'=2,'core'=2] {'zl','x','y','zh'}, dimensions={0} | all-to-all | bytes 3407872 | tf_op jit(solution)/shard_map/all_to_all | solution.py:280
  83.5 0.1 convert_reduce_fusion
  83.6 0.1 collective-permute-start
  83.7 1.2 %collective-permute-done = f32[40,128]{1,0:T(8,128)S(1)} collective-permute-done((f32[40,128]{1,0:T(8,128)S(1)}, f32[40,128]{1,0:T(8,128)S(1)}, u32[]{:S(2)}, u32[]{:S(2)}) %collective-permute-start) | collective-permute-done | bytes 20512 | tf_op jit(solution)/shard_map/ppermute | solution.py:282
  84.9 0.1 broadcast_in_dim.3
  85.0 19.8 %all_to_all.17.sums = bf16[64,40,128]{2,1,0:T(8,128)(2,1)S(1)} all-to-all(bf16[64,40,128]{2,1,0:T(8,128)(2,1)S(1)} %broadcast_in_dim.3), channel_id=1, replica_groups=mesh['zl'=2,'x'=4,'y'=4,'zh'=2,'core'=2] {'zl','x','y','zh'}, dimensions={0} | all-to-all | bytes 1310720 | tf_op jit(solution)/shard_map/all_to_all | solution.py:284
  104.8 1.9 %place_results.1 = (bf16[64,32,256]{2,1,0:T(8,128)(2,1)}, f32[256,768]{1,0:T(8,128)}, f32[256,256]{1,0:T(8,128)}, f32[512,64]{1,0:T(8,128)}, f32[1,256]{1,0:T(1,128)}) custom-call(bf16[64,104,128]{2,1,0:T(8,128)(2,1)S(1)} %all_to_all.16.y, bf16[64,40,128]{2,1,0:T(8,128)(2,1)S(1)} %all_to_all.17.sums, f32[1,256]{1,0:T(1,128)S(1)} %bitcast.9, ...), custom_call_target="tpu_custom_call" | custom-call | tf_op jit(solution)/shard_map/place_results/pallas_call | solution.py:252
  (1 shorter events, 0.0 us)
Async XLA Ops:
  2.4 41.2 %copy-start = (bf16[256,768]{1,0:T(8,128)(2,1)S(1)}, bf16[256,768]{1,0:T(8,128)(2,1)}, u32[]{:S(2)}) copy-start(bf16[256,768]{1,0:T(8,128)(2,1)} %wqkv.3) | copy-start | bytes 1179652
  2.4 41.2 %copy-start.1 = (f32[8,64,64]{2,1,0:T(8,128)S(1)}, f32[8,64,64]{2,1,0:T(8,128)}, u32[]{:S(2)}) copy-start(f32[8,64,64]{2,1,0:T(8,128)} %param.11) | copy-start | bytes 393220
  2.4 41.2 %copy-start.2 = (bf16[256,256]{1,0:T(8,128)(2,1)S(1)}, bf16[256,256]{1,0:T(8,128)(2,1)}, u32[]{:S(2)}) copy-start(bf16[256,256]{1,0:T(8,128)(2,1)} %wout.1) | copy-start | bytes 393220
  2.4 41.2 %copy-start.3 = (f32[256]{0:T(256)S(1)}, f32[256]{0:T(256)}, u32[]{:S(2)}) copy-start(f32[256]{0:T(256)} %param.8) | copy-start | bytes 3076
  83.6 1.3 %collective-permute-start = (f32[40,128]{1,0:T(8,128)S(1)}, f32[40,128]{1,0:T(8,128)S(1)}, u32[]{:S(2)}, u32[]{:S(2)}) collective-permute-start(f32[40,128]{1,0:T(8,128)S(1)} %convert_reduce_fusion), channel_id=1, source_target_pairs={{0,1},{1,0},{2,3},{3,2},{4,5},{5,4},{6,7},{7,6},{8,9},{9,8},{10,11... | collective-permute-start | bytes 61448 | tf_op jit(solution)/shard_map/ppermute | solution.py:282

commit v6 on v5

--- a/solution.py
+++ b/solution.py
@@ -160,18 +160,6 @@
         return 0
 
     lax.fori_loop(0, GROUPS // 8, attend, 0, unroll=4)
-    grad_qkv = dot(normed_s[...], gp_s[...], TN)
-    grad_proj = dot(att_s[...], dy_s[...], TN)
-    for t in range(6):
-        rows_s[256 * t : 256 * (t + 1), :] = grad_qkv[:, 128 * t : 128 * (t + 1)]
-    for t in range(2):
-        rows_s[256 * (6 + t) : 256 * (7 + t), :] = grad_proj[:, 128 * t : 128 * (t + 1)]
-    for t in range(4):
-        rows_s[2048 + 64 * t : 2112 + 64 * t, :] = grad_bias[:, 128 * t : 128 * (t + 1)]
-    rows_s[SHARES * SHARE :, :] = jnp.zeros((HELD - SHARE, 128), F32)
-    for d in range(SHARES):
-        msg[d, 2 * GROUPS :, :] = rows_s[SHARE * d : SHARE * d + HELD, :].astype(BF)
-
     def pull_back(b, _):
         rows = pl.ds(pl.multiple_of(b * 512, 512), 512)
         g = dot(gp_s[rows, :], wqkv[...], NT) * gain[...]
@@ -188,6 +176,18 @@
         return 0
 
     lax.fori_loop(0, GROUPS // 8, pull_back, 0, unroll=4)
+
+    grad_qkv = dot(normed_s[...], gp_s[...], TN)
+    grad_proj = dot(att_s[...], dy_s[...], TN)
+    for t in range(6):
+        rows_s[256 * t : 256 * (t + 1), :] = grad_qkv[:, 128 * t : 128 * (t + 1)]
+    for t in range(2):
+        rows_s[256 * (6 + t) : 256 * (7 + t), :] = grad_proj[:, 128 * t : 128 * (t + 1)]
+    for t in range(4):
+        rows_s[2048 + 64 * t : 2112 + 64 * t, :] = grad_bias[:, 128 * t : 128 * (t + 1)]
+    rows_s[SHARES * SHARE :, :] = jnp.zeros((HELD - SHARE, 128), F32)
+    for d in range(SHARES):
+        msg[d, 2 * GROUPS :, :] = rows_s[SHARE * d : SHARE * d + HELD, :].astype(BF)
 
     def write(s, _):
         for i, ref in enumerate((x0, x1)):

time: 107 us -> 107 us (level)
  no operation moved by 1% of the time
where the time goes in v6:
time: 107 us
  blocking collectives  90.2 us (84%)
  Pallas kernels  12.4 us (12%)
  other arithmetic  1.88 us (2%)
  waiting for transfers between devices  1.18 us (1%)
    all_to_all x1, blocking collectives, on_device(): arrived = lax.all_to_all(both, CHIPS, 0, 0, tiled=True)  41.2 us
    all_to_all x1, blocking collectives, on_device(): returned = lax.all_to_all(message, CHIPS, 0, 0, tiled=True)  29.3 us
    all_to_all x1, blocking collectives, on_device(): sums = lax.all_to_all(total, CHIPS, 0, 0, tiled=True)  19.8 us
    pallas_call x1, Pallas kernels, gradients(): pl.pallas_call(gradients_kernel, out_shape=jax.ShapeDtypeStruct((MEMBERS,...  10.5 us
  transfers between devices with their start and end apart: 1, of which 1 were waited for; matrix products, arithmetic and copies ran while one was open for 0% of the time, Pallas kernels for 0%

profile of v6, /device:TPU:0, one launch (start us, length us, event | category | flops | bytes accessed | tf_op | source)
XLA Modules:
  0.0 106.6 jit_solution(5657707331534867173)
XLA Ops:
  0.6 1.8 %pad_maximum_fusion = bf16[64,64,256]{2,1,0:T(8,128)(2,1)S(1)} fusion(bf16[64,32,256]{2,1,0:T(8,128)(2,1)} %bitcast.10, bf16[64,32,256]{2,1,0:T(8,128)(2,1)} %bitcast.11), kind=kLoop, calls=%fused_computation | loop fusion | flops 4194304 | bytes 4194304 | tf_op jit(solution)/shard_map/concatenate | solution.py:274
  2.4 0.0 copy-start
  2.4 0.0 copy-start.1
  2.4 0.0 copy-start.2
  2.4 0.0 copy-start.3
  2.4 41.2 %all_to_all.15.recv = bf16[64,64,256]{2,1,0:T(8,128)(2,1)S(1)} all-to-all(bf16[64,64,256]{2,1,0:T(8,128)(2,1)S(1)} %pad_maximum_fusion), channel_id=1, replica_groups=mesh['zl'=2,'x'=4,'y'=4,'zh'=2,'core'=2] {'zl','x','y','zh'}, dimensions={0} | all-to-all | bytes 4194304 | tf_op jit(solution)/shard_map/all_to_all | solution.py:277
  43.6 0.0 copy-done
  43.6 0.0 copy-done.1
  43.6 0.0 copy-done.2
  43.6 0.0 copy-done.3
  43.6 10.5 %layer_gradients.1 = bf16[64,104,128]{2,1,0:T(8,128)(2,1)S(1)} custom-call(bf16[64,64,256]{2,1,0:T(8,128)(2,1)S(1)} %all_to_all.15.recv, f32[1,256]{1,0:T(1,128)S(1)} %bitcast.8, bf16[256,768]{1,0:T(8,128)(2,1)S(1)} %copy-done, bf16[256,256]{1,0:T(8,128)(2,1)S(1)} %copy-done.2, f32[512,64]{1,0:T(8,128)S(1)} %bitcast.7), custom_call_target="tpu_custom_call" | custom-call | tf_op jit(solution)/shard_map/layer_gradients/pallas_call | solution.py:201
  54.1 29.3 %all_to_all.16.y = bf16[64,104,128]{2,1,0:T(8,128)(2,1)S(1)} all-to-all(bf16[64,104,128]{2,1,0:T(8,128)(2,1)S(1)} %layer_gradients.1), channel_id=1, replica_groups=mesh['zl'=2,'x'=4,'y'=4,'zh'=2,'core'=2] {'zl','x','y','zh'}, dimensions={0} | all-to-all | bytes 3407872 | tf_op jit(solution)/shard_map/all_to_all | solution.py:280
  83.4 0.1 convert_reduce_fusion
  83.5 0.1 collective-permute-start
  83.6 1.2 %collective-permute-done = f32[40,128]{1,0:T(8,128)S(1)} collective-permute-done((f32[40,128]{1,0:T(8,128)S(1)}, f32[40,128]{1,0:T(8,128)S(1)}, u32[]{:S(2)}, u32[]{:S(2)}) %collective-permute-start) | collective-permute-done | bytes 20512 | tf_op jit(solution)/shard_map/ppermute | solution.py:282
  84.8 0.1 broadcast_in_dim.3
  84.9 19.8 %all_to_all.17.sums = bf16[64,40,128]{2,1,0:T(8,128)(2,1)S(1)} all-to-all(bf16[64,40,128]{2,1,0:T(8,128)(2,1)S(1)} %broadcast_in_dim.3), channel_id=1, replica_groups=mesh['zl'=2,'x'=4,'y'=4,'zh'=2,'core'=2] {'zl','x','y','zh'}, dimensions={0} | all-to-all | bytes 1310720 | tf_op jit(solution)/shard_map/all_to_all | solution.py:284
  104.7 1.9 %place_results.1 = (bf16[64,32,256]{2,1,0:T(8,128)(2,1)}, f32[256,768]{1,0:T(8,128)}, f32[256,256]{1,0:T(8,128)}, f32[512,64]{1,0:T(8,128)}, f32[1,256]{1,0:T(1,128)}) custom-call(bf16[64,104,128]{2,1,0:T(8,128)(2,1)S(1)} %all_to_all.16.y, bf16[64,40,128]{2,1,0:T(8,128)(2,1)S(1)} %all_to_all.17.sums, f32[1,256]{1,0:T(1,128)S(1)} %bitcast.9, ...), custom_call_target="tpu_custom_call" | custom-call | tf_op jit(solution)/shard_map/place_results/pallas_call | solution.py:252
  (1 shorter events, 0.0 us)
Async XLA Ops:
  2.4 41.2 %copy-start = (bf16[256,768]{1,0:T(8,128)(2,1)S(1)}, bf16[256,768]{1,0:T(8,128)(2,1)}, u32[]{:S(2)}) copy-start(bf16[256,768]{1,0:T(8,128)(2,1)} %wqkv.3) | copy-start | bytes 1179652
  2.4 41.2 %copy-start.1 = (f32[8,64,64]{2,1,0:T(8,128)S(1)}, f32[8,64,64]{2,1,0:T(8,128)}, u32[]{:S(2)}) copy-start(f32[8,64,64]{2,1,0:T(8,128)} %param.11) | copy-start | bytes 393220
  2.4 41.2 %copy-start.2 = (bf16[256,256]{1,0:T(8,128)(2,1)S(1)}, bf16[256,256]{1,0:T(8,128)(2,1)}, u32[]{:S(2)}) copy-start(bf16[256,256]{1,0:T(8,128)(2,1)} %wout.1) | copy-start | bytes 393220
  2.4 41.2 %copy-start.3 = (f32[256]{0:T(256)S(1)}, f32[256]{0:T(256)}, u32[]{:S(2)}) copy-start(f32[256]{0:T(256)} %param.8) | copy-start | bytes 3076
  83.5 1.3 %collective-permute-start = (f32[40,128]{1,0:T(8,128)S(1)}, f32[40,128]{1,0:T(8,128)S(1)}, u32[]{:S(2)}, u32[]{:S(2)}) collective-permute-start(f32[40,128]{1,0:T(8,128)S(1)} %convert_reduce_fusion), channel_id=1, source_target_pairs={{0,1},{1,0},{2,3},{3,2},{4,5},{5,4},{6,7},{7,6},{8,9},{9,8},{10,11... | collective-permute-start | bytes 61448 | tf_op jit(solution)/shard_map/ppermute | solution.py:282

commit v7 on v6

--- a/solution.py
+++ b/solution.py
@@ -161,21 +161,21 @@
 
     lax.fori_loop(0, GROUPS // 8, attend, 0, unroll=4)
     def pull_back(b, _):
-        rows = pl.ds(pl.multiple_of(b * 512, 512), 512)
+        rows = pl.ds(pl.multiple_of(b * 1024, 1024), 1024)
         g = dot(gp_s[rows, :], wqkv[...], NT) * gain[...]
         normal = normal_s[rows, :]
         inverse = jnp.concatenate([inverse_s[rows, :]] * 2, axis=1)
         along = jnp.mean(g * normal, -1, keepdims=True)
         dx = inverse * (g - jnp.mean(g, -1, keepdims=True) - normal * along)
         dx = dy_s[rows, :].astype(F32) + dx
-        for k in range(8):
+        for k in range(16):
             for i, ref in enumerate((x0, x1)):
-                ref[pl.ds(b * 8 + k, MEMBERS, stride=STRIDE), :] = dx[
+                ref[pl.ds(b * 16 + k, MEMBERS, stride=STRIDE), :] = dx[
                     MEMBERS * k : MEMBERS * (k + 1), 128 * i : 128 * (i + 1)
                 ]
         return 0
 
-    lax.fori_loop(0, GROUPS // 8, pull_back, 0, unroll=4)
+    lax.fori_loop(0, GROUPS // 16, pull_back, 0, unroll=2)
 
     grad_qkv = dot(normed_s[...], gp_s[...], TN)
     grad_proj = dot(att_s[...], dy_s[...], TN)

time: 107 us -> 107 us (level)
  no operation moved by 1% of the time
where the time goes in v7:
time: 107 us
  blocking collectives  90.2 us (84%)
  Pallas kernels  12.5 us (12%)
  other arithmetic  1.88 us (2%)
  waiting for transfers between devices  1.18 us (1%)
    all_to_all x1, blocking collectives, on_device(): arrived = lax.all_to_all(both, CHIPS, 0, 0, tiled=True)  41.2 us
    all_to_all x1, blocking collectives, on_device(): returned = lax.all_to_all(message, CHIPS, 0, 0, tiled=True)  29.3 us
    all_to_all x1, blocking collectives, on_device(): sums = lax.all_to_all(total, CHIPS, 0, 0, tiled=True)  19.8 us
    pallas_call x1, Pallas kernels, gradients(): pl.pallas_call(gradients_kernel, out_shape=jax.ShapeDtypeStruct((MEMBERS,...  10.5 us
  transfers between devices with their start and end apart: 1, of which 1 were waited for; matrix products, arithmetic and copies ran while one was open for 0% of the time, Pallas kernels for 0%

profile of v7, /device:TPU:0, one launch (start us, length us, event | category | flops | bytes accessed | tf_op | source)
XLA Modules:
  0.0 106.7 jit_solution(1394308759394069144)
XLA Ops:
  0.6 1.8 %pad_maximum_fusion = bf16[64,64,256]{2,1,0:T(8,128)(2,1)S(1)} fusion(bf16[64,32,256]{2,1,0:T(8,128)(2,1)} %bitcast.10, bf16[64,32,256]{2,1,0:T(8,128)(2,1)} %bitcast.11), kind=kLoop, calls=%fused_computation | loop fusion | flops 4194304 | bytes 4194304 | tf_op jit(solution)/shard_map/concatenate | solution.py:274
  2.4 0.0 copy-start
  2.4 0.0 copy-start.1
  2.4 0.0 copy-start.2
  2.4 0.0 copy-start.3
  2.4 41.2 %all_to_all.15.recv = bf16[64,64,256]{2,1,0:T(8,128)(2,1)S(1)} all-to-all(bf16[64,64,256]{2,1,0:T(8,128)(2,1)S(1)} %pad_maximum_fusion), channel_id=1, replica_groups=mesh['zl'=2,'x'=4,'y'=4,'zh'=2,'core'=2] {'zl','x','y','zh'}, dimensions={0} | all-to-all | bytes 4194304 | tf_op jit(solution)/shard_map/all_to_all | solution.py:277
  43.6 0.0 copy-done
  43.6 0.0 copy-done.1
  43.6 0.0 copy-done.2
  43.6 0.0 copy-done.3
  43.6 10.5 %layer_gradients.1 = bf16[64,104,128]{2,1,0:T(8,128)(2,1)S(1)} custom-call(bf16[64,64,256]{2,1,0:T(8,128)(2,1)S(1)} %all_to_all.15.recv, f32[1,256]{1,0:T(1,128)S(1)} %bitcast.8, bf16[256,768]{1,0:T(8,128)(2,1)S(1)} %copy-done, bf16[256,256]{1,0:T(8,128)(2,1)S(1)} %copy-done.2, f32[512,64]{1,0:T(8,128)S(1)} %bitcast.7), custom_call_target="tpu_custom_call" | custom-call | tf_op jit(solution)/shard_map/layer_gradients/pallas_call | solution.py:201
  54.2 29.3 %all_to_all.16.y = bf16[64,104,128]{2,1,0:T(8,128)(2,1)S(1)} all-to-all(bf16[64,104,128]{2,1,0:T(8,128)(2,1)S(1)} %layer_gradients.1), channel_id=1, replica_groups=mesh['zl'=2,'x'=4,'y'=4,'zh'=2,'core'=2] {'zl','x','y','zh'}, dimensions={0} | all-to-all | bytes 3407872 | tf_op jit(solution)/shard_map/all_to_all | solution.py:280
  83.4 0.1 convert_reduce_fusion
  83.6 0.1 collective-permute-start
  83.6 1.2 %collective-permute-done = f32[40,128]{1,0:T(8,128)S(1)} collective-permute-done((f32[40,128]{1,0:T(8,128)S(1)}, f32[40,128]{1,0:T(8,128)S(1)}, u32[]{:S(2)}, u32[]{:S(2)}) %collective-permute-start) | collective-permute-done | bytes 20512 | tf_op jit(solution)/shard_map/ppermute | solution.py:282
  84.8 0.1 broadcast_in_dim.3
  84.9 19.8 %all_to_all.17.sums = bf16[64,40,128]{2,1,0:T(8,128)(2,1)S(1)} all-to-all(bf16[64,40,128]{2,1,0:T(8,128)(2,1)S(1)} %broadcast_in_dim.3), channel_id=1, replica_groups=mesh['zl'=2,'x'=4,'y'=4,'zh'=2,'core'=2] {'zl','x','y','zh'}, dimensions={0} | all-to-all | bytes 1310720 | tf_op jit(solution)/shard_map/all_to_all | solution.py:284
  104.8 1.9 %place_results.1 = (bf16[64,32,256]{2,1,0:T(8,128)(2,1)}, f32[256,768]{1,0:T(8,128)}, f32[256,256]{1,0:T(8,128)}, f32[512,64]{1,0:T(8,128)}, f32[1,256]{1,0:T(1,128)}) custom-call(bf16[64,104,128]{2,1,0:T(8,128)(2,1)S(1)} %all_to_all.16.y, bf16[64,40,128]{2,1,0:T(8,128)(2,1)S(1)} %all_to_all.17.sums, f32[1,256]{1,0:T(1,128)S(1)} %bitcast.9, ...), custom_call_target="tpu_custom_call" | custom-call | tf_op jit(solution)/shard_map/place_results/pallas_call | solution.py:252
  (1 shorter events, 0.0 us)
Async XLA Ops:
  2.4 41.2 %copy-start = (bf16[256,768]{1,0:T(8,128)(2,1)S(1)}, bf16[256,768]{1,0:T(8,128)(2,1)}, u32[]{:S(2)}) copy-start(bf16[256,768]{1,0:T(8,128)(2,1)} %wqkv.3) | copy-start | bytes 1179652
  2.4 41.2 %copy-start.1 = (f32[8,64,64]{2,1,0:T(8,128)S(1)}, f32[8,64,64]{2,1,0:T(8,128)}, u32[]{:S(2)}) copy-start(f32[8,64,64]{2,1,0:T(8,128)} %param.11) | copy-start | bytes 393220
  2.4 41.2 %copy-start.2 = (bf16[256,256]{1,0:T(8,128)(2,1)S(1)}, bf16[256,256]{1,0:T(8,128)(2,1)}, u32[]{:S(2)}) copy-start(bf16[256,256]{1,0:T(8,128)(2,1)} %wout.1) | copy-start | bytes 393220
  2.4 41.2 %copy-start.3 = (f32[256]{0:T(256)S(1)}, f32[256]{0:T(256)}, u32[]{:S(2)}) copy-start(f32[256]{0:T(256)} %param.8) | copy-start | bytes 3076
  83.6 1.3 %collective-permute-start = (f32[40,128]{1,0:T(8,128)S(1)}, f32[40,128]{1,0:T(8,128)S(1)}, u32[]{:S(2)}, u32[]{:S(2)}) collective-permute-start(f32[40,128]{1,0:T(8,128)S(1)} %convert_reduce_fusion), channel_id=1, source_target_pairs={{0,1},{1,0},{2,3},{3,2},{4,5},{5,4},{6,7},{7,6},{8,9},{9,8},{10,11... | collective-permute-start | bytes 61448 | tf_op jit(solution)/shard_map/ppermute | solution.py:282

commit v8 on v6

--- a/solution.py
+++ b/solution.py
@@ -226,7 +226,7 @@
         dx[s, :, 128:256] = y[s, 32:64, :]
         return 0
 
-    lax.fori_loop(0, 64, step, 0, unroll=8)
+    lax.fori_loop(0, 64, step, 0, unroll=64)
     for d in range(SHARES):
         share = sums[d].astype(F32)
         row = SHARE * d

time: 107 us -> 107 us (level)
  no operation moved by 1% of the time
where the time goes in v8:
time: 107 us
  blocking collectives  90.2 us (84%)
  Pallas kernels  12.4 us (12%)
  other arithmetic  1.88 us (2%)
  waiting for transfers between devices  1.18 us (1%)
    all_to_all x1, blocking collectives, on_device(): arrived = lax.all_to_all(both, CHIPS, 0, 0, tiled=True)  41.2 us
    all_to_all x1, blocking collectives, on_device(): returned = lax.all_to_all(message, CHIPS, 0, 0, tiled=True)  29.3 us
    all_to_all x1, blocking collectives, on_device(): sums = lax.all_to_all(total, CHIPS, 0, 0, tiled=True)  19.8 us
    pallas_call x1, Pallas kernels, gradients(): pl.pallas_call(gradients_kernel, out_shape=jax.ShapeDtypeStruct((MEMBERS,...  10.5 us
  transfers between devices with their start and end apart: 1, of which 1 were waited for; matrix products, arithmetic and copies ran while one was open for 0% of the time, Pallas kernels for 0%

profile of v8, /device:TPU:0, one launch (start us, length us, event | category | flops | bytes accessed | tf_op | source)
XLA Modules:
  0.0 106.6 jit_solution(14489978940303036710)
XLA Ops:
  0.6 1.8 %pad_maximum_fusion = bf16[64,64,256]{2,1,0:T(8,128)(2,1)S(1)} fusion(bf16[64,32,256]{2,1,0:T(8,128)(2,1)} %bitcast.10, bf16[64,32,256]{2,1,0:T(8,128)(2,1)} %bitcast.11), kind=kLoop, calls=%fused_computation | loop fusion | flops 4194304 | bytes 4194304 | tf_op jit(solution)/shard_map/concatenate | solution.py:274
  2.4 0.0 copy-start
  2.4 0.0 copy-start.1
  2.4 0.0 copy-start.2
  2.4 0.0 copy-start.3
  2.4 41.2 %all_to_all.15.recv = bf16[64,64,256]{2,1,0:T(8,128)(2,1)S(1)} all-to-all(bf16[64,64,256]{2,1,0:T(8,128)(2,1)S(1)} %pad_maximum_fusion), channel_id=1, replica_groups=mesh['zl'=2,'x'=4,'y'=4,'zh'=2,'core'=2] {'zl','x','y','zh'}, dimensions={0} | all-to-all | bytes 4194304 | tf_op jit(solution)/shard_map/all_to_all | solution.py:277
  43.6 0.0 copy-done
  43.6 0.0 copy-done.1
  43.6 0.0 copy-done.2
  43.6 0.0 copy-done.3
  43.6 10.5 %layer_gradients.1 = bf16[64,104,128]{2,1,0:T(8,128)(2,1)S(1)} custom-call(bf16[64,64,256]{2,1,0:T(8,128)(2,1)S(1)} %all_to_all.15.recv, f32[1,256]{1,0:T(1,128)S(1)} %bitcast.8, bf16[256,768]{1,0:T(8,128)(2,1)S(1)} %copy-done, bf16[256,256]{1,0:T(8,128)(2,1)S(1)} %copy-done.2, f32[512,64]{1,0:T(8,128)S(1)} %bitcast.7), custom_call_target="tpu_custom_call" | custom-call | tf_op jit(solution)/shard_map/layer_gradients/pallas_call | solution.py:201
  54.1 29.3 %all_to_all.16.y = bf16[64,104,128]{2,1,0:T(8,128)(2,1)S(1)} all-to-all(bf16[64,104,128]{2,1,0:T(8,128)(2,1)S(1)} %layer_gradients.1), channel_id=1, replica_groups=mesh['zl'=2,'x'=4,'y'=4,'zh'=2,'core'=2] {'zl','x','y','zh'}, dimensions={0} | all-to-all | bytes 3407872 | tf_op jit(solution)/shard_map/all_to_all | solution.py:280
  83.4 0.1 convert_reduce_fusion
  83.5 0.1 collective-permute-start
  83.6 1.2 %collective-permute-done = f32[40,128]{1,0:T(8,128)S(1)} collective-permute-done((f32[40,128]{1,0:T(8,128)S(1)}, f32[40,128]{1,0:T(8,128)S(1)}, u32[]{:S(2)}, u32[]{:S(2)}) %collective-permute-start) | collective-permute-done | bytes 20512 | tf_op jit(solution)/shard_map/ppermute | solution.py:282
  84.8 0.1 broadcast_in_dim.3
  84.9 19.8 %all_to_all.17.sums = bf16[64,40,128]{2,1,0:T(8,128)(2,1)S(1)} all-to-all(bf16[64,40,128]{2,1,0:T(8,128)(2,1)S(1)} %broadcast_in_dim.3), channel_id=1, replica_groups=mesh['zl'=2,'x'=4,'y'=4,'zh'=2,'core'=2] {'zl','x','y','zh'}, dimensions={0} | all-to-all | bytes 1310720 | tf_op jit(solution)/shard_map/all_to_all | solution.py:284
  104.7 1.9 %place_results.1 = (bf16[64,32,256]{2,1,0:T(8,128)(2,1)}, f32[256,768]{1,0:T(8,128)}, f32[256,256]{1,0:T(8,128)}, f32[512,64]{1,0:T(8,128)}, f32[1,256]{1,0:T(1,128)}) custom-call(bf16[64,104,128]{2,1,0:T(8,128)(2,1)S(1)} %all_to_all.16.y, bf16[64,40,128]{2,1,0:T(8,128)(2,1)S(1)} %all_to_all.17.sums, f32[1,256]{1,0:T(1,128)S(1)} %bitcast.9, ...), custom_call_target="tpu_custom_call" | custom-call | tf_op jit(solution)/shard_map/place_results/pallas_call | solution.py:252
  (1 shorter events, 0.0 us)
Async XLA Ops:
  2.4 41.2 %copy-start = (bf16[256,768]{1,0:T(8,128)(2,1)S(1)}, bf16[256,768]{1,0:T(8,128)(2,1)}, u32[]{:S(2)}) copy-start(bf16[256,768]{1,0:T(8,128)(2,1)} %wqkv.3) | copy-start | bytes 1179652
  2.4 41.2 %copy-start.1 = (f32[8,64,64]{2,1,0:T(8,128)S(1)}, f32[8,64,64]{2,1,0:T(8,128)}, u32[]{:S(2)}) copy-start(f32[8,64,64]{2,1,0:T(8,128)} %param.11) | copy-start | bytes 393220
  2.4 41.2 %copy-start.2 = (bf16[256,256]{1,0:T(8,128)(2,1)S(1)}, bf16[256,256]{1,0:T(8,128)(2,1)}, u32[]{:S(2)}) copy-start(bf16[256,256]{1,0:T(8,128)(2,1)} %wout.1) | copy-start | bytes 393220
  2.4 41.2 %copy-start.3 = (f32[256]{0:T(256)S(1)}, f32[256]{0:T(256)}, u32[]{:S(2)}) copy-start(f32[256]{0:T(256)} %param.8) | copy-start | bytes 3076
  83.5 1.3 %collective-permute-start = (f32[40,128]{1,0:T(8,128)S(1)}, f32[40,128]{1,0:T(8,128)S(1)}, u32[]{:S(2)}, u32[]{:S(2)}) collective-permute-start(f32[40,128]{1,0:T(8,128)S(1)} %convert_reduce_fusion), channel_id=1, source_target_pairs={{0,1},{1,0},{2,3},{3,2},{4,5},{5,4},{6,7},{7,6},{8,9},{9,8},{10,11... | collective-permute-start | bytes 61448 | tf_op jit(solution)/shard_map/ppermute | solution.py:282
